TPU v7x, 1024 devices: a whole 4x8x16 slice. The times are simulated.
1024 devices in a mesh: section: 16 (over x, y_lo), expert: 64 (over z, y_hi, core).
Axes of the slice: x: 4, y: 8 (y_hi: 2, y_lo: 4; y = y_hi * 4 + y_lo), z: 16, core: 2. Of those that a mesh axis runs over, the one named last changes fastest.
Arguments:
- forward_handoff: bfloat16 [16, 1024, 3584], P('section', 'expert'), may hold values from -6 to 6
- backward_handoff: bfloat16 [16, 1024, 3584], P('section', 'expert'), may hold values from -6 to 6
- forward_routes: int32 [16, 1024, 2], P('section', 'expert'), may hold values from 0 to 7, all different within a row; in each aligned block of 16 rows (0 to 15, 16 to 31, ..., all dimensions but the last counted through in order) at most 4 rows name the same one
- backward_routes: int32 [16, 1024, 2], P('section', 'expert'), may hold values from 0 to 7, all different within a row; in each aligned block of 16 rows (0 to 15, 16 to 31, ..., all dimensions but the last counted through in order) at most 4 rows name the same one
- forward_gates: float32 [16, 1024, 2], P('section', 'expert'), may hold values from 0.2 to 1.4
- backward_gates: float32 [16, 1024, 2], P('section', 'expert'), may hold values from 0.2 to 1.4
- gate_weight: bfloat16 [16, 3584, 8192], P('section', None, 'expert'), may hold values from -0.09375 to 0.09375
- up_weight: bfloat16 [16, 3584, 8192], P('section', None, 'expert'), may hold values from -0.09375 to 0.09375
- down_weight: bfloat16 [16, 8192, 3584], P('section', 'expert'), may hold values from -0.1875 to 0.1875
- saved_gate: bfloat16 [16, 256, 8192], P('section', None, 'expert'), may hold values from -5 to 5
- saved_up: bfloat16 [16, 256, 8192], P('section', None, 'expert'), may hold values from -5 to 5
Outputs:
- forward_out: bfloat16 [16, 1024, 3584], P('section', 'expert')
- backward_out: bfloat16 [16, 1024, 3584], P('section', 'expert')
Inputs may be any that keep to these rules, and one draw needn't show every extreme that they name: `forward_routes`: each token names 2 different experts. In the rows of one index of expert (aligned blocks of 16 tokens) no expert is named more than 4 times, and some block names some expert exactly 4 times. `backward_routes`: each token names 2 different experts. In the rows of one index of expert (aligned blocks of 16 tokens) no expert is named more than 4 times, and some block names some expert exactly 4 times.
All inputs are finite; a program needn't handle non-finite values.
Results may differ from a plain program's by a relative error of at most 0.0054.
Values may be sent and summed in bfloat16 or wider, within the bound.
No kernel may reach another device: no remote copies, remote signals or barrier semaphores. Data moves between devices by JAX's collectives and lax.ppermute only.
A program may use at most 64 MiB of HBM per device.

v0:
```python
import jax
import jax.numpy as jnp
from jax import lax
from jax.sharding import PartitionSpec as P

EXPERTS = 8


def from_behind(x, axis, by):
    count = lax.axis_size(axis)
    return lax.ppermute(x, axis, [(i, (i + by) % count) for i in range(count)])


def slot_tables(routes, experts, shards, capacity):
    count_rows = routes.shape[0]
    expert_ids = jnp.arange(experts, dtype=jnp.int32)
    chosen = (routes[:, :, None] == expert_ids[None, None, :]).astype(jnp.int32)
    chosen_any = jnp.sum(chosen, axis=1)
    position = jnp.cumsum(chosen_any, axis=0) - chosen_any
    placed = (position[:, :, None] == jnp.arange(capacity, dtype=jnp.int32)[None, None, :]).astype(
        jnp.int32
    )
    tables = []
    for column in range(routes.shape[1]):
        single = chosen[:, column, :, None] * placed
        spread = jnp.broadcast_to(single[:, :, None, :], (count_rows, experts, shards, capacity))
        tables.append(spread.reshape(count_rows, experts * shards * capacity).astype(jnp.bfloat16))
    return tables


def gather_slots(tables, rows_list):
    total = None
    for table, rows in zip(tables, rows_list):
        term = lax.dot_general(
            table, rows, (((0,), (0,)), ((), ())), preferred_element_type=jnp.float32
        )
        total = term if total is None else total + term
    return total.astype(jnp.bfloat16)


def on_device(
    forward_handoff,
    backward_handoff,
    forward_routes,
    backward_routes,
    forward_gates,
    backward_gates,
    gate_weight,
    up_weight,
    down_weight,
    saved_gate,
    saved_up,
):
    devices_expert = lax.axis_size("expert")
    experts = EXPERTS
    shards = devices_expert // experts
    capacity = saved_gate.shape[1] // devices_expert
    arrive = from_behind(forward_handoff, "section", 1)[0]
    grad = from_behind(backward_handoff, "section", -1)[0]
    fwd_tables = slot_tables(forward_routes[0], experts, shards, capacity)
    bwd_tables = slot_tables(backward_routes[0], experts, shards, capacity)
    fwd_weights = forward_gates[0]
    bwd_weights = backward_gates[0]
    topk_count = len(fwd_tables)
    grad_wide = grad.astype(jnp.float32)
    scaled_rows = [
        (bwd_weights[:, column : column + 1] * grad_wide).astype(jnp.bfloat16)
        for column in range(topk_count)
    ]
    backward_send = gather_slots(bwd_tables, scaled_rows)
    gate_local = gate_weight[0]
    up_local = up_weight[0]
    down_local = down_weight[0]
    kept_gate = saved_gate[0].astype(jnp.float32)
    kept_up = saved_up[0].astype(jnp.float32)
    contract_last = (((1,), (1,)), ((), ()))
    forward_send = gather_slots(fwd_tables, [arrive] * topk_count)
    received = lax.all_to_all(forward_send, "expert", split_axis=0, concat_axis=0, tiled=True)
    pre_gate = jnp.dot(received, gate_local, preferred_element_type=jnp.float32)
    pre_up = jnp.dot(received, up_local, preferred_element_type=jnp.float32)
    hidden = (jax.nn.silu(pre_gate) * pre_up).astype(jnp.bfloat16)
    forward_ret = lax.all_to_all(
        jnp.dot(hidden, down_local, preferred_element_type=jnp.float32).astype(jnp.bfloat16),
        "expert",
        split_axis=0,
        concat_axis=0,
        tiled=True,
    )
    received = lax.all_to_all(backward_send, "expert", split_axis=0, concat_axis=0, tiled=True)
    grad_hidden = lax.dot_general(
        received, down_local, contract_last, preferred_element_type=jnp.float32
    )
    sigma = jax.nn.sigmoid(kept_gate)
    d_gate = (grad_hidden * kept_up * sigma * (1.0 + kept_gate * (1.0 - sigma))).astype(
        jnp.bfloat16
    )
    d_up = (grad_hidden * kept_gate * sigma).astype(jnp.bfloat16)
    result = lax.dot_general(d_gate, gate_local, contract_last, preferred_element_type=jnp.float32)
    result = result + lax.dot_general(
        d_up, up_local, contract_last, preferred_element_type=jnp.float32
    )
    backward_ret = lax.all_to_all(
        result.astype(jnp.bfloat16), "expert", split_axis=0, concat_axis=0, tiled=True
    )
    forward_total = arrive.astype(jnp.float32)
    backward_total = grad_wide
    for column in range(topk_count):
        forward_total = forward_total + fwd_weights[:, column : column + 1] * jnp.dot(
            fwd_tables[column], forward_ret, preferred_element_type=jnp.float32
        )
        backward_total = backward_total + jnp.dot(
            bwd_tables[column], backward_ret, preferred_element_type=jnp.float32
        )
    return (forward_total.astype(jnp.bfloat16)[None], backward_total.astype(jnp.bfloat16)[None])


def solution(mesh):
    return jax.shard_map(
        on_device,
        mesh=mesh,
        in_specs=(
            P("section", "expert", None),
            P("section", "expert", None),
            P("section", "expert", None),
            P("section", "expert", None),
            P("section", "expert", None),
            P("section", "expert", None),
            P("section", None, "expert"),
            P("section", None, "expert"),
            P("section", "expert", None),
            P("section", None, "expert"),
            P("section", None, "expert"),
        ),
        out_specs=(P("section", "expert", None), P("section", "expert", None)),
        check_vma=False,
    )
```

profile of v0, /device:TPU:62, one launch (start us, length us, event | category | flops | bytes accessed | tf_op | source)
XLA Modules:
  0.0 430.1 jit_solution(1010610228228704225)
XLA Ops:
  0.6 3.4 collective-permute-start.1
  4.0 0.7 fusion.55
  4.7 0.7 fusion.54
  5.6 0.8 slice_bitcast_fusion.5
  6.4 5.3 %collective-permute-done.1 = bf16[1,16,3584]{2,1,0:T(8,128)(2,1)S(1)} collective-permute-done((bf16[1,16,3584]{2,1,0:T(8,128)(2,1)}, bf16[1,16,3584]{2,1,0:T(8,128)(2,1)S(1)}, u32[]{:S(2)}, u32[]{:S(2)}) %collective-permute-start.1) | collective-permute-done | bytes 114720 | tf_op jit(solution)/shard_map/ppermute | solution.py:11
  11.7 0.7 fusion.35
  12.4 0.7 fusion.2
  13.1 1.5 all_to_all.38
  14.6 24.8 %all-to-all-start.2 = ((bf16[64,4,3584]{2,1,0:T(4,128)(2,1)}), bf16[64,4,3584]{2,1,0:T(4,128)(2,1)S(1)}, u32[]{:S(2)}, u32[]{:S(2)}) async-start(bf16[64,4,3584]{2,1,0:T(4,128)(2,1)} %all_to_all.38), calls=%async_computation.2 | async-start | bytes 3670016 | tf_op jit(solution)/shard_map/all_to_all | solution.py:89
  39.4 1.9 collective-permute-start
  41.6 5.8 %collective-permute-done = bf16[1,16,3584]{2,1,0:T(8,128)(2,1)S(1)} collective-permute-done((bf16[1,16,3584]{2,1,0:T(8,128)(2,1)S(1)}, bf16[1,16,3584]{2,1,0:T(8,128)(2,1)S(1)}, u32[]{:S(2)}, u32[]{:S(2)}) %collective-permute-start) | collective-permute-done | bytes 114720 | tf_op jit(solution)/shard_map/ppermute | solution.py:11
  48.0 1.9 fusion.1
  49.8 4.1 all_to_all.32
  53.9 75.2 %all-to-all-done.2 = bf16[64,4,3584]{2,1,0:T(4,128)(2,1)S(1)} async-done(((bf16[64,4,3584]{2,1,0:T(4,128)(2,1)}), bf16[64,4,3584]{2,1,0:T(4,128)(2,1)S(1)}, u32[]{:S(2)}, u32[]{:S(2)}) %all-to-all-start.2) | async-done | bytes 1835040 | tf_op jit(solution)/shard_map/all_to_all | solution.py:89
  129.2 7.9 %all-to-all-start = ((bf16[64,4,3584]{2,1,0:T(4,128)(2,1)}), bf16[64,4,3584]{2,1,0:T(4,128)(2,1)}, u32[]{:S(2)}, u32[]{:S(2)}) async-start(bf16[64,4,3584]{2,1,0:T(4,128)(2,1)} %all_to_all.32), calls=%async_computation | async-start | bytes 3670016 | tf_op jit(solution)/shard_map/all_to_all | solution.py:78
  137.1 1.5 all_to_all.40
  138.6 2.4 fusion.4
  142.4 1.5 all_to_all.41
  143.8 83.0 %all-to-all-done = bf16[64,4,3584]{2,1,0:T(4,128)(2,1)} async-done(((bf16[64,4,3584]{2,1,0:T(4,128)(2,1)}), bf16[64,4,3584]{2,1,0:T(4,128)(2,1)}, u32[]{:S(2)}, u32[]{:S(2)}) %all-to-all-start) | async-done | bytes 1835040 | tf_op jit(solution)/shard_map/all_to_all | solution.py:78
  226.8 7.9 %all-to-all-start.3 = ((bf16[64,4,3584]{2,1,0:T(4,128)(2,1)}), bf16[64,4,3584]{2,1,0:T(4,128)(2,1)}, u32[]{:S(2)}, u32[]{:S(2)}) async-start(bf16[64,4,3584]{2,1,0:T(4,128)(2,1)} %all_to_all.41), calls=%async_computation.3 | async-start | bytes 3670016 | tf_op jit(solution)/shard_map/all_to_all | solution.py:102
  234.7 2.9 all_to_all.34
  237.7 1.8 fusion.12
  239.5 3.6 convolution_convert_fusion
  243.1 4.1 all_to_all.35
  247.2 77.3 %all-to-all-done.3 = bf16[64,4,3584]{2,1,0:T(4,128)(2,1)} async-done(((bf16[64,4,3584]{2,1,0:T(4,128)(2,1)}), bf16[64,4,3584]{2,1,0:T(4,128)(2,1)}, u32[]{:S(2)}, u32[]{:S(2)}) %all-to-all-start.3) | async-done | bytes 1835040 | tf_op jit(solution)/shard_map/all_to_all | solution.py:102
  324.5 7.9 %all-to-all-start.1 = ((bf16[64,4,3584]{2,1,0:T(4,128)(2,1)}), bf16[64,4,3584]{2,1,0:T(4,128)(2,1)}, u32[]{:S(2)}, u32[]{:S(2)}) async-start(bf16[64,4,3584]{2,1,0:T(4,128)(2,1)} %all_to_all.35), calls=%async_computation.1 | async-start | bytes 3670016 | tf_op jit(solution)/shard_map/all_to_all | solution.py:82
  332.4 2.9 all_to_all.43
  335.7 86.4 %all-to-all-done.1 = bf16[64,4,3584]{2,1,0:T(4,128)(2,1)} async-done(((bf16[64,4,3584]{2,1,0:T(4,128)(2,1)}), bf16[64,4,3584]{2,1,0:T(4,128)(2,1)}, u32[]{:S(2)}, u32[]{:S(2)}) %all-to-all-start.1) | async-done | bytes 1835040 | tf_op jit(solution)/shard_map/all_to_all | solution.py:82
  422.1 4.0 all_to_all.37
  426.1 2.0 convolution_multiply_fusion.1
  428.1 1.0 fusion.39
  429.1 1.0 fusion.33
  (39 shorter events, 2.8 us)
Async XLA Ops:
  0.6 141.1 %copy-start = (bf16[1,3584,128]{2,1,0:T(8,128)(2,1)S(1)}, bf16[1,3584,128]{2,1,0:T(8,128)(2,1)}, u32[]{:S(2)}) copy-start(bf16[1,3584,128]{2,1,0:T(8,128)(2,1)} %param.18) | copy-start | bytes 2752516
  0.6 11.0 %collective-permute-start.1 = (bf16[1,16,3584]{2,1,0:T(8,128)(2,1)}, bf16[1,16,3584]{2,1,0:T(8,128)(2,1)S(1)}, u32[]{:S(2)}, u32[]{:S(2)}) collective-permute-start(bf16[1,16,3584]{2,1,0:T(8,128)(2,1)} %param.12), channel_id=1, source_target_pairs={{0,960},{64,0},{128,64},{192,128},{256,192},{320,256},{384,320},{4... | collective-permute-start | bytes 344072 | tf_op jit(solution)/shard_map/ppermute | solution.py:11
  14.6 24.8 %copy-start.7 = (bf16[1,16,3584]{2,1,0:T(8,128)(2,1)S(1)}, bf16[1,16,3584]{2,1,0:T(8,128)(2,1)}, u32[]{:S(2)}) copy-start(bf16[1,16,3584]{2,1,0:T(8,128)(2,1)} %param.11) | copy-start | bytes 344068
  14.6 26.8 %copy-start.5 = (s32[1,16,2]{1,2,0:T(2,128)S(1)}, s32[1,16,2]{1,2,0:T(2,128)}, u32[]{:S(2)}) copy-start(s32[1,16,2]{1,2,0:T(2,128)} %param.13) | copy-start | bytes 388
  14.6 114.6 %all-to-all-start.2 = ((bf16[64,4,3584]{2,1,0:T(4,128)(2,1)}), bf16[64,4,3584]{2,1,0:T(4,128)(2,1)S(1)}, u32[]{:S(2)}, u32[]{:S(2)}) async-start(bf16[64,4,3584]{2,1,0:T(4,128)(2,1)} %all_to_all.38), calls=%async_computation.2 | async-start | bytes 3670016 | tf_op jit(solution)/shard_map/all_to_all | solution.py:89
  39.4 7.9 %collective-permute-start = (bf16[1,16,3584]{2,1,0:T(8,128)(2,1)S(1)}, bf16[1,16,3584]{2,1,0:T(8,128)(2,1)S(1)}, u32[]{:S(2)}, u32[]{:S(2)}) collective-permute-start(bf16[1,16,3584]{2,1,0:T(8,128)(2,1)S(1)} %copy-done.7), channel_id=1, source_target_pairs={{0,64},{64,128},{128,192},{192,256},{256,320},{320,384},{384,448},... | collective-permute-start | bytes 344072 | tf_op jit(solution)/shard_map/ppermute | solution.py:11
  129.2 97.7 %all-to-all-start = ((bf16[64,4,3584]{2,1,0:T(4,128)(2,1)}), bf16[64,4,3584]{2,1,0:T(4,128)(2,1)}, u32[]{:S(2)}, u32[]{:S(2)}) async-start(bf16[64,4,3584]{2,1,0:T(4,128)(2,1)} %all_to_all.32), calls=%async_computation | async-start | bytes 3670016 | tf_op jit(solution)/shard_map/all_to_all | solution.py:78
  138.6 2.5 copy-start.2
  138.6 2.5 copy-start.3
  138.6 2.5 copy-start.4
  226.8 97.7 %all-to-all-start.3 = ((bf16[64,4,3584]{2,1,0:T(4,128)(2,1)}), bf16[64,4,3584]{2,1,0:T(4,128)(2,1)}, u32[]{:S(2)}, u32[]{:S(2)}) async-start(bf16[64,4,3584]{2,1,0:T(4,128)(2,1)} %all_to_all.41), calls=%async_computation.3 | async-start | bytes 3670016 | tf_op jit(solution)/shard_map/all_to_all | solution.py:102
  247.2 85.2 %copy-start.6 = (f32[1,16,2]{1,2,0:T(2,128)S(1)}, f32[1,16,2]{1,2,0:T(2,128)}, u32[]{:S(2)}) copy-start(f32[1,16,2]{1,2,0:T(2,128)} %param.15) | copy-start | bytes 388
  324.5 97.7 %all-to-all-start.1 = ((bf16[64,4,3584]{2,1,0:T(4,128)(2,1)}), bf16[64,4,3584]{2,1,0:T(4,128)(2,1)}, u32[]{:S(2)}, u32[]{:S(2)}) async-start(bf16[64,4,3584]{2,1,0:T(4,128)(2,1)} %all_to_all.35), calls=%async_computation.1 | async-start | bytes 3670016 | tf_op jit(solution)/shard_map/all_to_all | solution.py:82
  426.1 3.0 copy-start.1
where the time goes:
time: 431 us; the launch traced here: 430 us
  waiting for transfers between devices  333 us (77%)
  starting transfers between devices  53.9 us (13%)
  local copies, waits for them, and re-layouts  23.6 us (5%)
  matrix products  17.4 us (4%)
    all_to_all x1, waiting for transfers between devices, on_device(): lax.all_to_all(jnp.dot(hidden, down_local, preferred_element_type=jnp.flo...  86.4 us
    all_to_all x1, waiting for transfers between devices, on_device(): lax.all_to_all(forward_send, 'expert', split_axis=0, concat_axis=0, tiled...  83 us
    all_to_all x1, waiting for transfers between devices, on_device(): lax.all_to_all(result.astype(jnp.bfloat16), 'expert', split_axis=0, conca...  77.3 us
    all_to_all x1, waiting for transfers between devices, on_device(): lax.all_to_all(backward_send, 'expert', split_axis=0, concat_axis=0, tile...  75.2 us
    all_to_all x1, starting transfers between devices, on_device(): lax.all_to_all(backward_send, 'expert', split_axis=0, concat_axis=0, tile...  24.8 us
    ppermute x2, waiting for transfers between devices, from_behind(): return lax.ppermute(x, axis, [(i, (i + by) % count) for i in range(count)])  11 us
  transfers between devices with their start and end apart: 6, of which 6 were waited for; matrix products, arithmetic and copies ran while one was open for 3% of the time, Pallas kernels for 0%

commit v1 on v0

v1 whole, which is shorter than its diff:
```python
import jax
import jax.numpy as jnp
import numpy as np
from jax import lax
from jax.sharding import PartitionSpec as P

EXPERTS = 8
CHUNKS = 1
CORE, Y_HI, Z_LO = 1, 2, 4


def from_behind(x, axis, by):
    count = lax.axis_size(axis)
    return lax.ppermute(x, axis, [(i, (i + by) % count) for i in range(count)])


def swap(x, bit):
    count = lax.axis_size("expert")
    return lax.ppermute(x, "expert", [(i, i ^ bit) for i in range(count)])


def across_experts(x, shards):
    groups = [[e * shards + w for e in range(EXPERTS)] for w in range(shards)]
    return lax.all_to_all(
        x, "expert", split_axis=0, concat_axis=0, tiled=True, axis_index_groups=groups
    )


def places(routes, capacity):
    ids = jnp.arange(EXPERTS, dtype=jnp.int32)
    chosen = (routes[:, :, None] == ids).astype(jnp.int32)
    chosen_any = jnp.sum(chosen, axis=1)
    rows = routes.shape[0]
    before = (jnp.arange(rows)[:, None] > jnp.arange(rows)[None, :]).astype(jnp.int32)
    position = jnp.sum(before[:, :, None] * chosen_any[None], axis=1)
    placed = (position[:, :, None] == jnp.arange(capacity, dtype=jnp.int32)).astype(jnp.int32)
    return [chosen[:, k, :, None] * placed for k in range(routes.shape[1])]


def saved_slots(own, shards, capacity):
    rows = []
    per = EXPERTS // CHUNKS
    for part in range(CHUNKS):
        for peer in (0, Y_HI, Z_LO, Y_HI | Z_LO):
            for e in range(part * per, (part + 1) * per):
                for back in (0, 1):
                    for c in range(capacity):
                        rows.append((peer, e, back, c))
    peer, e, back, c = (jnp.asarray(x, jnp.int32) for x in np.array(rows).T)
    return (e * shards + ((own % shards) ^ peer)) * capacity + c, back


def on_device(
    forward_handoff,
    backward_handoff,
    forward_routes,
    backward_routes,
    forward_gates,
    backward_gates,
    gate_weight,
    up_weight,
    down_weight,
    saved_gate,
    saved_up,
):
    shards = lax.axis_size("expert") // EXPERTS
    own = lax.axis_index("expert")
    capacity = saved_gate.shape[1] // lax.axis_size("expert")
    bf16, f32 = jnp.bfloat16, jnp.float32
    hold = lax.optimization_barrier
    arrive = from_behind(forward_handoff[0], "section", 1)
    grad = from_behind(backward_handoff[0], "section", -1)
    tokens, width = arrive.shape
    tile = 2 * capacity

    fwd = places(forward_routes[0], capacity)
    bwd = places(backward_routes[0], capacity)
    zero = jnp.zeros_like(fwd[0])

    def spread(forward, backward):
        both = jnp.stack([forward, backward], axis=2)
        return both.reshape(tokens, EXPERTS * tile).astype(bf16)

    send_table = jnp.concatenate(
        [spread(fwd[0] + fwd[1], zero), spread(zero, bwd[0]), spread(zero, bwd[1])], axis=0
    )
    back_table = jnp.concatenate(
        [spread(fwd[0], zero), spread(fwd[1], zero), spread(zero, bwd[0] + bwd[1])], axis=0
    )
    send_table, back_table = hold((send_table, back_table))

    grad_wide = grad.astype(f32)
    scaled = [(backward_gates[0][:, k : k + 1] * grad_wide).astype(bf16) for k in range(2)]
    rows_in = jnp.concatenate([arrive] + scaled, axis=0)
    first = (((0,), (0,)), ((), ()))
    send = lax.dot_general(send_table, rows_in, first, preferred_element_type=f32).astype(bf16)

    send, gate_local, up_local, down_local, both_saved = hold(
        (
            send,
            gate_weight[0],
            up_weight[0],
            down_weight[0],
            jnp.concatenate([saved_gate[0], saved_up[0]], axis=1),
        )
    )
    got = across_experts(send, shards)
    count = got.shape[0] // CHUNKS

    units = down_local.shape[0]
    weights = hold(jnp.concatenate([gate_local, up_local, down_local.T], axis=1))
    weights = [weights, swap(weights, CORE)]

    def saved_for(device):
        slot, is_back = saved_slots(device, shards, capacity)
        pick = (slot[:, None] == jnp.arange(saved_gate.shape[1])) & (is_back[:, None] == 1)
        return jnp.dot(pick.astype(bf16), both_saved, preferred_element_type=f32).astype(bf16)

    saved = [saved_for(own), swap(saved_for(own ^ CORE), CORE)]
    slopes = []
    for pair in saved:
        g, u = pair[:, :units].astype(f32), pair[:, units:].astype(f32)
        sigma = jax.nn.sigmoid(g)
        slopes.append(hold((u * sigma * (1.0 + g * (1.0 - sigma)), g * sigma)))

    def results(rows, part):
        n = rows.shape[0]
        at = slice(part * n, (part + 1) * n)
        of_forward = (lax.broadcasted_iota(jnp.int32, (n, units), 0) // capacity) % 2 == 0
        last = (((1,), (1,)), ((), ()))
        total = None
        for weight, (slope_gate, slope_up) in zip(weights, slopes):
            pre = jnp.dot(rows, weight, preferred_element_type=f32)
            h = jnp.where(of_forward, jax.nn.silu(pre[:, :units]) * pre[:, units : 2 * units], 0.0)
            dh = pre[:, 2 * units :]
            columns = [dh * slope_gate[at], dh * slope_up[at], h]
            hidden = hold(jnp.concatenate([x.astype(bf16) for x in columns], axis=1))
            term = lax.dot_general(hidden, weight, last, preferred_element_type=f32)
            total = term if total is None else total + term
        return total

    at_z = swap(got, Z_LO)
    near = []
    for part in range(CHUNKS):
        own_rows = slice(part * count, (part + 1) * count)
        at_y = swap(got[own_rows], Y_HI)
        at_zy = swap(at_y, Z_LO)
        near.append(jnp.concatenate([got[own_rows], at_y, at_z[own_rows], at_zy], axis=0))

    done = []
    for part, rows in enumerate(near):
        here = results(rows, part)
        at = [here[i * count : (i + 1) * count] for i in range(4)]
        from_zy = swap(at[3].astype(bf16), Z_LO)
        from_y = swap((at[1] + from_zy.astype(f32)).astype(bf16), Y_HI)
        from_z = swap(at[2].astype(bf16), Z_LO)
        done.append((at[0] + from_z.astype(f32) + from_y.astype(f32)).astype(bf16))
    back = across_experts(jnp.concatenate(done, axis=0), shards)
    sums = jnp.dot(back_table, back, preferred_element_type=f32)
    gates = forward_gates[0]
    forward_out = (
        arrive.astype(f32)
        + gates[:, 0:1] * sums[:tokens]
        + gates[:, 1:2] * sums[tokens : 2 * tokens]
    )
    backward_out = grad_wide + sums[2 * tokens :]
    return (forward_out.astype(bf16)[None], backward_out.astype(bf16)[None])


def solution(mesh):
    return jax.shard_map(
        on_device,
        mesh=mesh,
        in_specs=(
            P("section", "expert", None),
            P("section", "expert", None),
            P("section", "expert", None),
            P("section", "expert", None),
            P("section", "expert", None),
            P("section", "expert", None),
            P("section", None, "expert"),
            P("section", None, "expert"),
            P("section", "expert", None),
            P("section", None, "expert"),
            P("section", None, "expert"),
        ),
        out_specs=(P("section", "expert", None), P("section", "expert", None)),
        check_vma=False,
    )
```

time: 431 us -> 188 us (0.44)
  the two profiles are of different devices: /device:TPU:62 before, /device:TPU:64 now
where the time goes in v1:
time: 188 us; the launch traced here: 187 us
  waiting for transfers between devices  102 us (54%)
  starting transfers between devices  62.5 us (33%)
  matrix products  9.93 us (5%)
  other arithmetic  7.31 us (4%)
  local copies, waits for them, and re-layouts  4.64 us (2%)
    all_to_all x2, waiting for transfers between devices, across_experts(): lax.all_to_all(x, 'expert', split_axis=0, concat_axis=0, tiled=True, axis...  50.4 us
    ppermute x8, waiting for transfers between devices, swap(): return lax.ppermute(x, 'expert', [(i, i ^ bit) for i in range(count)])  50.3 us
    all_to_all x2, starting transfers between devices, across_experts(): lax.all_to_all(x, 'expert', split_axis=0, concat_axis=0, tiled=True, axis...  30.4 us
    ppermute x8, starting transfers between devices, swap(): return lax.ppermute(x, 'expert', [(i, i ^ bit) for i in range(count)])  22.4 us
    ppermute x2, starting transfers between devices, from_behind(): return lax.ppermute(x, axis, [(i, (i + by) % count) for i in range(count)])  9.76 us
    dot_general x2, matrix products, results(): term = lax.dot_general(hidden, weight, last, preferred_element_type=f32)  4.12 us
    dot_general x2, matrix products, results(): pre = jnp.dot(rows, weight, preferred_element_type=f32)  4.02 us
  transfers between devices with their start and end apart: 12, of which 8 were waited for; matrix products, arithmetic and copies ran while one was open for 7% of the time, Pallas kernels for 0%

profile of v1, /device:TPU:64, one launch (start us, length us, event | category | flops | bytes accessed | tf_op | source)
XLA Modules:
  0.0 187.4 jit_solution(9905202997121796736)
XLA Ops:
  0.7 7.8 %collective-permute-start.1 = (bf16[16,3584]{1,0:T(8,128)(2,1)}, bf16[16,3584]{1,0:T(8,128)(2,1)S(1)}, u32[]{:S(2)}, u32[]{:S(2)}) collective-permute-start(bf16[16,3584]{1,0:T(8,128)(2,1)} %bitcast.76), channel_id=1, source_target_pairs={{0,960},{64,0},{128,64},{192,128},{256,192},{320,256},{384,320},{4... | collective-permute-start | bytes 344072 | tf_op jit(solution)/shard_map/ppermute | solution.py:14
  8.5 1.9 %collective-permute-start = (bf16[16,3584]{1,0:T(8,128)(2,1)}, bf16[16,3584]{1,0:T(8,128)(2,1)S(1)}, u32[]{:S(2)}, u32[]{:S(2)}) collective-permute-start(bf16[16,3584]{1,0:T(8,128)(2,1)} %bitcast.77), channel_id=1, source_target_pairs={{0,64},{64,128},{128,192},{192,256},{256,320},{320,384},{384,448},... | collective-permute-start | bytes 344072 | tf_op jit(solution)/shard_map/ppermute | solution.py:14
  11.1 0.7 fusion.50
  13.6 0.8 slice_bitcast_fusion.6
  14.4 2.3 %copy.35 = bf16[1,3584,128]{1,2,0:T(8,128)(2,1)} copy(bf16[1,3584,128]{2,1,0:T(8,128)(2,1)} %param.25) | data formatting | bytes 1835008 | tf_op args[6]
  16.6 1.3 copy.36
  18.1 1.2 collective-permute-done
  19.3 1.0 convolution_convert_fusion
  20.3 17.9 %all-to-all-start = ((bf16[8,8,3584]{2,1,0:T(8,128)(2,1)}), bf16[8,8,3584]{2,1,0:T(8,128)(2,1)S(1)}, u32[]{:S(2)}, u32[]{:S(2)}) async-start(bf16[8,8,3584]{2,1,0:T(8,128)(2,1)} %bitcast.24), calls=%async_computation | async-start | bytes 917504 | tf_op jit(solution)/shard_map/all_to_all | solution.py:24
  38.2 1.9 %pad_maximum_fusion = bf16[3584,384]{0,1:T(8,128)(2,1)S(1)} fusion(bf16[3584,128]{0,1:T(8,128)(2,1)} %bitcast.57, bf16[3584,128]{0,1:T(8,128)(2,1)} %bitcast.56, bf16[3584,128]{0,1:T(8,128)(2,1)} %bitcast.55), kind=kLoop, calls=%fused_computation.2 | loop fusion | flops 8257536 | bytes 5505024 | tf_op jit(solution)/shard_map/concatenate | solution.py:111
  40.2 1.9 %collective-permute-start.5 = (bf16[3584,384]{0,1:T(8,128)(2,1)S(1)}, bf16[3584,384]{0,1:T(8,128)(2,1)}, u32[]{:S(2)}, u32[]{:S(2)}) collective-permute-start(bf16[3584,384]{0,1:T(8,128)(2,1)S(1)} %pad_maximum_fusion), channel_id=1, source_target_pairs={{0,1},{1,0},{2,3},{3,2},{4,5},{5,4},{6,7},{7,6},{8,9},{9,8},{10,11... | collective-permute-start | bytes 8257544 | tf_op jit(solution)/shard_map/ppermute | solution.py:19
  42.2 22.5 %all-to-all-done = bf16[8,8,3584]{2,1,0:T(8,128)(2,1)S(1)} async-done(((bf16[8,8,3584]{2,1,0:T(8,128)(2,1)}), bf16[8,8,3584]{2,1,0:T(8,128)(2,1)S(1)}, u32[]{:S(2)}, u32[]{:S(2)}) %all-to-all-start) | async-done | bytes 458784 | tf_op jit(solution)/shard_map/all_to_all | solution.py:24
  64.7 5.0 %collective-permute-start.2 = (bf16[64,3584]{1,0:T(8,128)(2,1)S(1)}, bf16[64,3584]{1,0:T(8,128)(2,1)S(1)}, u32[]{:S(2)}, u32[]{:S(2)}) collective-permute-start(bf16[64,3584]{1,0:T(8,128)(2,1)S(1)} %bitcast.58), channel_id=1, source_target_pairs={{0,2},{1,3},{2,0},{3,1},{4,6},{5,7},{6,4},{7,5},{8,10},{9,11},{10,... | collective-permute-start | bytes 1376264 | tf_op jit(solution)/shard_map/ppermute | solution.py:19
  70.0 1.9 %collective-permute-start.6 = (bf16[256,256]{1,0:T(8,128)(2,1)S(1)}, bf16[256,256]{1,0:T(8,128)(2,1)S(1)}, u32[]{:S(2)}, u32[]{:S(2)}) collective-permute-start(bf16[256,256]{1,0:T(8,128)(2,1)S(1)} %convolution_convert_fusion.1), channel_id=1, source_target_pairs={{0,1},{1,0},{2,3},{3,2},{4,5},{5,4},{6,7},{7,6},{8,9},{9,8},{10,11... | collective-permute-start | bytes 393224 | tf_op jit(solution)/shard_map/ppermute | solution.py:19
  72.2 1.9 %collective-permute-start.3 = (bf16[64,3584]{1,0:T(8,128)(2,1)S(1)}, bf16[64,3584]{1,0:T(8,128)(2,1)S(1)}, u32[]{:S(2)}, u32[]{:S(2)}) collective-permute-start(bf16[64,3584]{1,0:T(8,128)(2,1)S(1)} %bitcast.59), channel_id=1, source_target_pairs={{0,4},{1,5},{2,6},{3,7},{4,0},{5,1},{6,2},{7,3},{8,12},{9,13},{10,... | collective-permute-start | bytes 1376264 | tf_op jit(solution)/shard_map/ppermute | solution.py:19
  74.2 14.3 %collective-permute-done.2 = bf16[64,3584]{1,0:T(8,128)(2,1)S(1)} collective-permute-done((bf16[64,3584]{1,0:T(8,128)(2,1)S(1)}, bf16[64,3584]{1,0:T(8,128)(2,1)S(1)}, u32[]{:S(2)}, u32[]{:S(2)}) %collective-permute-start.2) | collective-permute-done | bytes 458784 | tf_op jit(solution)/shard_map/ppermute | solution.py:19
  88.5 1.9 %collective-permute-start.4 = (bf16[64,3584]{1,0:T(8,128)(2,1)S(1)}, bf16[64,3584]{1,0:T(8,128)(2,1)S(1)}, u32[]{:S(2)}, u32[]{:S(2)}) collective-permute-start(bf16[64,3584]{1,0:T(8,128)(2,1)S(1)} %collective-permute-done.2), channel_id=1, source_target_pairs={{0,4},{1,5},{2,6},{3,7},{4,0},{5,1},{6,2},{7,3},{8,12},{9,13},{10,... | collective-permute-start | bytes 1376264 | tf_op jit(solution)/shard_map/ppermute | solution.py:19
  90.6 12.2 %collective-permute-done.4 = bf16[64,3584]{1,0:T(8,128)(2,1)S(1)} collective-permute-done((bf16[64,3584]{1,0:T(8,128)(2,1)S(1)}, bf16[64,3584]{1,0:T(8,128)(2,1)S(1)}, u32[]{:S(2)}, u32[]{:S(2)}) %collective-permute-start.4) | collective-permute-done | bytes 458784 | tf_op jit(solution)/shard_map/ppermute | solution.py:19
  102.8 1.1 fusion.12
  104.2 1.1 fusion.59
  105.3 2.9 %fusion.11 = f32[256,384]{1,0:T(8,128)S(1)} fusion(bf16[3584,384]{0,1:T(8,128)(2,1)} %collective-permute-done.5, bf16[64,3584]{1,0:T(8,128)(2,1)S(1)} %collective-permute-done.4, bf16[64,3584]{1,0:T(8,128)(2,1)S(1)} %collective-permute-done.3, bf16[64,3584]{1,0:T(8,128)(2,1)S(1)} %collective-permute-done.2, bf16[64,3584]{1,0:T(8,128)(2,1)S(1)} %bitcast.61), kind=kOutput, calls=%fused_computation.22 | convolution fusion | flops 711983104 | bytes 4980736 | tf_op jit(solution)/shard_map/dot_general | solution.py:133
  108.4 3.0 %fusion.58 = (bf16[256,3584]{1,0:T(8,128)(2,1)S(1)}, f32[256,3584]{1,0:T(8,128)S(1)}) fusion(f32[256,3584]{1,0:T(8,128)S(1)} %fusion.59, bf16[256,384]{1,0:T(8,128)(2,1)S(1)} %pad_maximum_fusion.5, bf16[3584,384]{0,1:T(8,128)(2,1)} %collective-permute-done.5), kind=kOutput, calls=%fused_computation.121 | convolution fusion | flops 706478080 | bytes 12124160 | tf_op jit(solution)/shard_map/dot_general | solution.py:138
  111.5 2.2 %collective-permute-start.8 = (bf16[64,3584]{1,0:T(8,128)(2,1)S(1)}, bf16[64,3584]{1,0:T(8,128)(2,1)S(1)}, u32[]{:S(2)}, u32[]{:S(2)}) collective-permute-start(bf16[64,3584]{1,0:T(8,128)(2,1)S(1)} %get-tuple-element.27), channel_id=1, source_target_pairs={{0,4},{1,5},{2,6},{3,7},{4,0},{5,1},{6,2},{7,3},{8,12},{9,13},{10,... | collective-permute-start | bytes 1376264 | tf_op jit(solution)/shard_map/ppermute | solution.py:19
  113.7 3.6 %collective-permute-start.7 = (bf16[64,3584]{1,0:T(8,128)(2,1)S(1)}, bf16[64,3584]{1,0:T(8,128)(2,1)S(1)}, u32[]{:S(2)}, u32[]{:S(2)}) collective-permute-start(bf16[64,3584]{1,0:T(8,128)(2,1)S(1)} %get-tuple-element.26), channel_id=1, source_target_pairs={{0,4},{1,5},{2,6},{3,7},{4,0},{5,1},{6,2},{7,3},{8,12},{9,13},{10,... | collective-permute-start | bytes 1376264 | tf_op jit(solution)/shard_map/ppermute | solution.py:19
  117.4 9.5 %collective-permute-done.8 = bf16[64,3584]{1,0:T(8,128)(2,1)S(1)} collective-permute-done((bf16[64,3584]{1,0:T(8,128)(2,1)S(1)}, bf16[64,3584]{1,0:T(8,128)(2,1)S(1)}, u32[]{:S(2)}, u32[]{:S(2)}) %collective-permute-start.8) | collective-permute-done | bytes 458784 | tf_op jit(solution)/shard_map/ppermute | solution.py:19
  127.0 3.8 %collective-permute-start.9 = (bf16[64,3584]{1,0:T(8,128)(2,1)S(1)}, bf16[64,3584]{1,0:T(8,128)(2,1)S(1)}, u32[]{:S(2)}, u32[]{:S(2)}) collective-permute-start(bf16[64,3584]{1,0:T(8,128)(2,1)S(1)} %fusion), channel_id=1, source_target_pairs={{0,2},{1,3},{2,0},{3,1},{4,6},{5,7},{6,4},{7,5},{8,10},{9,11},{10,... | collective-permute-start | bytes 1376264 | tf_op jit(solution)/shard_map/ppermute | solution.py:19
  130.8 4.0 %collective-permute-done.7 = bf16[64,3584]{1,0:T(8,128)(2,1)S(1)} collective-permute-done((bf16[64,3584]{1,0:T(8,128)(2,1)S(1)}, bf16[64,3584]{1,0:T(8,128)(2,1)S(1)}, u32[]{:S(2)}, u32[]{:S(2)}) %collective-permute-start.7) | collective-permute-done | bytes 458784 | tf_op jit(solution)/shard_map/ppermute | solution.py:19
  134.8 10.2 %collective-permute-done.9 = bf16[64,3584]{1,0:T(8,128)(2,1)S(1)} collective-permute-done((bf16[64,3584]{1,0:T(8,128)(2,1)S(1)}, bf16[64,3584]{1,0:T(8,128)(2,1)S(1)}, u32[]{:S(2)}, u32[]{:S(2)}) %collective-permute-start.9) | collective-permute-done | bytes 458784 | tf_op jit(solution)/shard_map/ppermute | solution.py:19
  145.0 0.9 fusion.3
  145.9 12.5 %all-to-all-start.1 = ((bf16[8,8,3584]{2,1,0:T(8,128)(2,1)}), bf16[8,8,3584]{2,1,0:T(8,128)(2,1)S(1)}, u32[]{:S(2)}, u32[]{:S(2)}) async-start(bf16[8,8,3584]{2,1,0:T(8,128)(2,1)} %fusion.3), calls=%async_computation.1 | async-start | bytes 917504 | tf_op jit(solution)/shard_map/all_to_all | solution.py:24
  158.5 27.9 %all-to-all-done.1 = bf16[8,8,3584]{2,1,0:T(8,128)(2,1)S(1)} async-done(((bf16[8,8,3584]{2,1,0:T(8,128)(2,1)}), bf16[8,8,3584]{2,1,0:T(8,128)(2,1)S(1)}, u32[]{:S(2)}, u32[]{:S(2)}) %all-to-all-start.1) | async-done | bytes 458784 | tf_op jit(solution)/shard_map/all_to_all | solution.py:24
  186.7 0.8 fusion.44
  (59 shorter events, 4.1 us)
Async XLA Ops:
  0.6 16.0 %copy-start = (bf16[1,3584,128]{2,1,0:T(8,128)(2,1)S(1)}, bf16[1,3584,128]{2,1,0:T(8,128)(2,1)}, u32[]{:S(2)}) copy-start(bf16[1,3584,128]{2,1,0:T(8,128)(2,1)} %param.26) | copy-start | bytes 2752516
  0.6 17.3 %copy-start.4 = (bf16[1,256,128]{2,1,0:T(8,128)(2,1)S(1)}, bf16[1,256,128]{2,1,0:T(8,128)(2,1)}, u32[]{:S(2)}) copy-start(bf16[1,256,128]{2,1,0:T(8,128)(2,1)} %param.28) | copy-start | bytes 196612
  0.7 17.3 %copy-start.3 = (bf16[1,256,128]{2,1,0:T(8,128)(2,1)S(1)}, bf16[1,256,128]{2,1,0:T(8,128)(2,1)}, u32[]{:S(2)}) copy-start(bf16[1,256,128]{2,1,0:T(8,128)(2,1)} %param.29) | copy-start | bytes 196612
  0.7 17.3 %collective-permute-start.1 = (bf16[16,3584]{1,0:T(8,128)(2,1)}, bf16[16,3584]{1,0:T(8,128)(2,1)S(1)}, u32[]{:S(2)}, u32[]{:S(2)}) collective-permute-start(bf16[16,3584]{1,0:T(8,128)(2,1)} %bitcast.76), channel_id=1, source_target_pairs={{0,960},{64,0},{128,64},{192,128},{256,192},{320,256},{384,320},{4... | collective-permute-start | bytes 344072 | tf_op jit(solution)/shard_map/ppermute | solution.py:14
  8.5 10.8 %collective-permute-start = (bf16[16,3584]{1,0:T(8,128)(2,1)}, bf16[16,3584]{1,0:T(8,128)(2,1)S(1)}, u32[]{:S(2)}, u32[]{:S(2)}) collective-permute-start(bf16[16,3584]{1,0:T(8,128)(2,1)} %bitcast.77), channel_id=1, source_target_pairs={{0,64},{64,128},{128,192},{192,256},{256,320},{320,384},{384,448},... | collective-permute-start | bytes 344072 | tf_op jit(solution)/shard_map/ppermute | solution.py:14
  19.3 18.9 %copy-start.1 = (bf16[16,3584]{1,0:T(8,128)(2,1)}, bf16[16,3584]{1,0:T(8,128)(2,1)S(1)}, u32[]{:S(2)}) copy-start(bf16[16,3584]{1,0:T(8,128)(2,1)S(1)} %collective-permute-done) | copy-start | bytes 344068
  20.3 44.4 %all-to-all-start = ((bf16[8,8,3584]{2,1,0:T(8,128)(2,1)}), bf16[8,8,3584]{2,1,0:T(8,128)(2,1)S(1)}, u32[]{:S(2)}, u32[]{:S(2)}) async-start(bf16[8,8,3584]{2,1,0:T(8,128)(2,1)} %bitcast.24), calls=%async_computation | async-start | bytes 917504 | tf_op jit(solution)/shard_map/all_to_all | solution.py:24
  38.2 4.0 %copy-start.6 = (s32[256]{0:T(256)S(1)}, s32[256]{0:T(256)}, u32[]{:S(2)}) copy-start(s32[256]{0:T(256)} %constant.108) | copy-start | bytes 3076
  38.2 4.0 %copy-start.7 = (s32[256]{0:T(256)S(1)}, s32[256]{0:T(256)}, u32[]{:S(2)}) copy-start(s32[256]{0:T(256)} %constant.81.clone) | copy-start | bytes 3076
  38.2 4.0 %copy-start.8 = (s32[256]{0:T(256)S(1)}, s32[256]{0:T(256)}, u32[]{:S(2)}) copy-start(s32[256]{0:T(256)} %constant.84.clone) | copy-start | bytes 3076
  38.2 31.5 %copy-start.9 = (pred[256]{0:T(512)(128)(4,1)S(1)}, pred[256]{0:T(512)(128)(4,1)}, u32[]{:S(2)}) copy-start(pred[256]{0:T(512)(128)(4,1)} %constant.109) | copy-start | bytes 772
  40.2 65.1 %collective-permute-start.5 = (bf16[3584,384]{0,1:T(8,128)(2,1)S(1)}, bf16[3584,384]{0,1:T(8,128)(2,1)}, u32[]{:S(2)}, u32[]{:S(2)}) collective-permute-start(bf16[3584,384]{0,1:T(8,128)(2,1)S(1)} %pad_maximum_fusion), channel_id=1, source_target_pairs={{0,1},{1,0},{2,3},{3,2},{4,5},{5,4},{6,7},{7,6},{8,9},{9,8},{10,11... | collective-permute-start | bytes 8257544 | tf_op jit(solution)/shard_map/ppermute | solution.py:19
  64.7 23.8 %collective-permute-start.2 = (bf16[64,3584]{1,0:T(8,128)(2,1)S(1)}, bf16[64,3584]{1,0:T(8,128)(2,1)S(1)}, u32[]{:S(2)}, u32[]{:S(2)}) collective-permute-start(bf16[64,3584]{1,0:T(8,128)(2,1)S(1)} %bitcast.58), channel_id=1, source_target_pairs={{0,2},{1,3},{2,0},{3,1},{4,6},{5,7},{6,4},{7,5},{8,10},{9,11},{10,... | collective-permute-start | bytes 1376264 | tf_op jit(solution)/shard_map/ppermute | solution.py:19
  70.0 20.5 %collective-permute-start.6 = (bf16[256,256]{1,0:T(8,128)(2,1)S(1)}, bf16[256,256]{1,0:T(8,128)(2,1)S(1)}, u32[]{:S(2)}, u32[]{:S(2)}) collective-permute-start(bf16[256,256]{1,0:T(8,128)(2,1)S(1)} %convolution_convert_fusion.1), channel_id=1, source_target_pairs={{0,1},{1,0},{2,3},{3,2},{4,5},{5,4},{6,7},{7,6},{8,9},{9,8},{10,11... | collective-permute-start | bytes 393224 | tf_op jit(solution)/shard_map/ppermute | solution.py:19
  72.2 18.4 %collective-permute-start.3 = (bf16[64,3584]{1,0:T(8,128)(2,1)S(1)}, bf16[64,3584]{1,0:T(8,128)(2,1)S(1)}, u32[]{:S(2)}, u32[]{:S(2)}) collective-permute-start(bf16[64,3584]{1,0:T(8,128)(2,1)S(1)} %bitcast.59), channel_id=1, source_target_pairs={{0,4},{1,5},{2,6},{3,7},{4,0},{5,1},{6,2},{7,3},{8,12},{9,13},{10,... | collective-permute-start | bytes 1376264 | tf_op jit(solution)/shard_map/ppermute | solution.py:19
  88.5 14.3 %collective-permute-start.4 = (bf16[64,3584]{1,0:T(8,128)(2,1)S(1)}, bf16[64,3584]{1,0:T(8,128)(2,1)S(1)}, u32[]{:S(2)}, u32[]{:S(2)}) collective-permute-start(bf16[64,3584]{1,0:T(8,128)(2,1)S(1)} %collective-permute-done.2), channel_id=1, source_target_pairs={{0,4},{1,5},{2,6},{3,7},{4,0},{5,1},{6,2},{7,3},{8,12},{9,13},{10,... | collective-permute-start | bytes 1376264 | tf_op jit(solution)/shard_map/ppermute | solution.py:19
  111.5 47.0 %copy-start.5 = (f32[1,16,2]{1,2,0:T(2,128)S(1)}, f32[1,16,2]{1,2,0:T(2,128)}, u32[]{:S(2)}) copy-start(f32[1,16,2]{1,2,0:T(2,128)} %param.23) | copy-start | bytes 388
  111.5 15.3 %collective-permute-start.8 = (bf16[64,3584]{1,0:T(8,128)(2,1)S(1)}, bf16[64,3584]{1,0:T(8,128)(2,1)S(1)}, u32[]{:S(2)}, u32[]{:S(2)}) collective-permute-start(bf16[64,3584]{1,0:T(8,128)(2,1)S(1)} %get-tuple-element.27), channel_id=1, source_target_pairs={{0,4},{1,5},{2,6},{3,7},{4,0},{5,1},{6,2},{7,3},{8,12},{9,13},{10,... | collective-permute-start | bytes 1376264 | tf_op jit(solution)/shard_map/ppermute | solution.py:19
  113.7 21.1 %collective-permute-start.7 = (bf16[64,3584]{1,0:T(8,128)(2,1)S(1)}, bf16[64,3584]{1,0:T(8,128)(2,1)S(1)}, u32[]{:S(2)}, u32[]{:S(2)}) collective-permute-start(bf16[64,3584]{1,0:T(8,128)(2,1)S(1)} %get-tuple-element.26), channel_id=1, source_target_pairs={{0,4},{1,5},{2,6},{3,7},{4,0},{5,1},{6,2},{7,3},{8,12},{9,13},{10,... | collective-permute-start | bytes 1376264 | tf_op jit(solution)/shard_map/ppermute | solution.py:19
  126.9 59.8 %copy-start.2 = (bf16[16,3584]{1,0:T(8,128)(2,1)S(1)}, bf16[16,3584]{1,0:T(8,128)(2,1)}, u32[]{:S(2)}) copy-start(bf16[16,3584]{1,0:T(8,128)(2,1)} %copy-done.1) | copy-start | bytes 344068
  127.0 18.0 %collective-permute-start.9 = (bf16[64,3584]{1,0:T(8,128)(2,1)S(1)}, bf16[64,3584]{1,0:T(8,128)(2,1)S(1)}, u32[]{:S(2)}, u32[]{:S(2)}) collective-permute-start(bf16[64,3584]{1,0:T(8,128)(2,1)S(1)} %fusion), channel_id=1, source_target_pairs={{0,2},{1,3},{2,0},{3,1},{4,6},{5,7},{6,4},{7,5},{8,10},{9,11},{10,... | collective-permute-start | bytes 1376264 | tf_op jit(solution)/shard_map/ppermute | solution.py:19
  145.9 40.4 %all-to-all-start.1 = ((bf16[8,8,3584]{2,1,0:T(8,128)(2,1)}), bf16[8,8,3584]{2,1,0:T(8,128)(2,1)S(1)}, u32[]{:S(2)}, u32[]{:S(2)}) async-start(bf16[8,8,3584]{2,1,0:T(8,128)(2,1)} %fusion.3), calls=%async_computation.1 | async-start | bytes 917504 | tf_op jit(solution)/shard_map/all_to_all | solution.py:24

commit v2 on v1

--- a/solution.py
+++ b/solution.py
@@ -1,12 +1,16 @@
+import functools
+
 import jax
 import jax.numpy as jnp
 import numpy as np
 from jax import lax
+from jax.experimental import pallas as pl
+from jax.experimental.pallas import tpu as pltpu
 from jax.sharding import PartitionSpec as P
 
 EXPERTS = 8
-CHUNKS = 1
 CORE, Y_HI, Z_LO = 1, 2, 4
+COLUMNS = 512
 
 
 def from_behind(x, axis, by):
@@ -38,16 +42,73 @@
 
 
 def saved_slots(own, shards, capacity):
-    rows = []
-    per = EXPERTS // CHUNKS
-    for part in range(CHUNKS):
-        for peer in (0, Y_HI, Z_LO, Y_HI | Z_LO):
-            for e in range(part * per, (part + 1) * per):
-                for back in (0, 1):
-                    for c in range(capacity):
-                        rows.append((peer, e, back, c))
+    rows = [
+        (peer, e, back, c)
+        for peer in (0, Y_HI, Z_LO, Y_HI | Z_LO)
+        for e in range(EXPERTS)
+        for back in (0, 1)
+        for c in range(capacity)
+    ]
     peer, e, back, c = (jnp.asarray(x, jnp.int32) for x in np.array(rows).T)
     return (e * shards + ((own % shards) ^ peer)) * capacity + c, back
+
+
+def expert_kernel(blocks, capacity, *refs):
+    sources, gates, ups, downs = refs[:blocks], *(refs[blocks + i : blocks + i + 2] for i in (0, 2, 4))
+    slope_gate, slope_up = refs[blocks + 6 : blocks + 8]
+    outs = refs[blocks + 8 : 2 * blocks + 8]
+    f32, bf16 = jnp.float32, jnp.bfloat16
+    n, width = sources[0].shape
+    units = gates[0].shape[1]
+    if blocks == 1:
+        rows = sources[0]
+    else:
+        rows = refs[-1]
+        for i, ref in enumerate(sources):
+            rows[i * n : (i + 1) * n] = ref[...]
+    last = (((1,), (1,)), ((), ()))
+    row = lax.broadcasted_iota(jnp.int32, (blocks * n, units), 0)
+    of_forward = lax.rem(lax.div(row, capacity), 2) == 0
+    hidden, d_gate, d_up = [], [], []
+    for i, (gate, up, down) in enumerate(zip(gates, ups, downs)):
+        pre_gate = jnp.dot(rows[...], gate[...], preferred_element_type=f32)
+        pre_up = jnp.dot(rows[...], up[...], preferred_element_type=f32)
+        d_hidden = lax.dot_general(rows[...], down[...], last, preferred_element_type=f32)
+        silu = pre_gate / (1.0 + jnp.exp(-pre_gate))
+        half = slice(i * units, (i + 1) * units)
+        hidden.append(jnp.where(of_forward, silu * pre_up, 0.0).astype(bf16))
+        d_gate.append((d_hidden * slope_gate[:, half]).astype(bf16))
+        d_up.append((d_hidden * slope_up[:, half]).astype(bf16))
+    for at in range(0, width, COLUMNS):
+        part = pl.ds(at, COLUMNS)
+        result = None
+        for i, (gate, up, down) in enumerate(zip(gates, ups, downs)):
+            term = jnp.dot(hidden[i], down[:, part], preferred_element_type=f32)
+            term += lax.dot_general(d_gate[i], gate[part], last, preferred_element_type=f32)
+            term += lax.dot_general(d_up[i], up[part], last, preferred_element_type=f32)
+            result = term if result is None else result + term
+        for i, ref in enumerate(outs):
+            ref[:, part] = result[i * n : (i + 1) * n].astype(ref.dtype)
+
+
+def through_expert(rows, kinds, weights, slopes, capacity):
+    blocks = len(rows)
+    n, width = rows[0].shape
+    units = weights[0].shape[1]
+    vmem = pl.BlockSpec(memory_space=pltpu.VMEM)
+    return pl.pallas_call(
+        functools.partial(expert_kernel, blocks, capacity),
+        out_shape=[jax.ShapeDtypeStruct((n, width), kind) for kind in kinds],
+        in_specs=[vmem] * (blocks + 8),
+        out_specs=[vmem] * blocks,
+        scratch_shapes=[pltpu.VMEM((blocks * n, width), jnp.bfloat16)] if blocks > 1 else [],
+        compiler_params=pltpu.CompilerParams(vmem_limit_bytes=32 * 1024 * 1024),
+        cost_estimate=pl.CostEstimate(
+            flops=24 * blocks * n * width * units,
+            bytes_accessed=12 * width * units + 6 * blocks * n * width,
+            transcendentals=2 * blocks * n * units,
+        ),
+    )(*rows, *weights, *slopes)
 
 
 def on_device(
@@ -95,21 +156,19 @@
     first = (((0,), (0,)), ((), ()))
     send = lax.dot_general(send_table, rows_in, first, preferred_element_type=f32).astype(bf16)
 
-    send, gate_local, up_local, down_local, both_saved = hold(
+    got = across_experts(send, shards)
+
+    got, gate, up, down, both_saved = hold(
         (
-            send,
+            got,
             gate_weight[0],
             up_weight[0],
             down_weight[0],
             jnp.concatenate([saved_gate[0], saved_up[0]], axis=1),
         )
     )
-    got = across_experts(send, shards)
-    count = got.shape[0] // CHUNKS
-
-    units = down_local.shape[0]
-    weights = hold(jnp.concatenate([gate_local, up_local, down_local.T], axis=1))
-    weights = [weights, swap(weights, CORE)]
+
+    weights = [w for mine in (gate, up, down) for w in (mine, swap(mine, CORE))]
 
     def saved_for(device):
         slot, is_back = saved_slots(device, shards, capacity)
@@ -117,47 +176,32 @@
         return jnp.dot(pick.astype(bf16), both_saved, preferred_element_type=f32).astype(bf16)
 
     saved = [saved_for(own), swap(saved_for(own ^ CORE), CORE)]
-    slopes = []
-    for pair in saved:
-        g, u = pair[:, :units].astype(f32), pair[:, units:].astype(f32)
-        sigma = jax.nn.sigmoid(g)
-        slopes.append(hold((u * sigma * (1.0 + g * (1.0 - sigma)), g * sigma)))
-
-    def results(rows, part):
-        n = rows.shape[0]
-        at = slice(part * n, (part + 1) * n)
-        of_forward = (lax.broadcasted_iota(jnp.int32, (n, units), 0) // capacity) % 2 == 0
-        last = (((1,), (1,)), ((), ()))
-        total = None
-        for weight, (slope_gate, slope_up) in zip(weights, slopes):
-            pre = jnp.dot(rows, weight, preferred_element_type=f32)
-            h = jnp.where(of_forward, jax.nn.silu(pre[:, :units]) * pre[:, units : 2 * units], 0.0)
-            dh = pre[:, 2 * units :]
-            columns = [dh * slope_gate[at], dh * slope_up[at], h]
-            hidden = hold(jnp.concatenate([x.astype(bf16) for x in columns], axis=1))
-            term = lax.dot_general(hidden, weight, last, preferred_element_type=f32)
-            total = term if total is None else total + term
-        return total
-
+    g, u = (
+        jnp.concatenate([x.astype(f32) for x in pair], axis=1)
+        for pair in zip(*(jnp.split(x, 2, axis=1) for x in saved))
+    )
+    sigma = jax.nn.sigmoid(g)
+    slopes = hold((u * sigma * (1.0 + g * (1.0 - sigma)), g * sigma))
+
+    at_y = swap(got, Y_HI)
     at_z = swap(got, Z_LO)
-    near = []
-    for part in range(CHUNKS):
-        own_rows = slice(part * count, (part + 1) * count)
-        at_y = swap(got[own_rows], Y_HI)
-        at_zy = swap(at_y, Z_LO)
-        near.append(jnp.concatenate([got[own_rows], at_y, at_z[own_rows], at_zy], axis=0))
-
-    done = []
-    for part, rows in enumerate(near):
-        here = results(rows, part)
-        at = [here[i * count : (i + 1) * count] for i in range(4)]
-        from_zy = swap(at[3].astype(bf16), Z_LO)
-        from_y = swap((at[1] + from_zy.astype(f32)).astype(bf16), Y_HI)
-        from_z = swap(at[2].astype(bf16), Z_LO)
-        done.append((at[0] + from_z.astype(f32) + from_y.astype(f32)).astype(bf16))
-    back = across_experts(jnp.concatenate(done, axis=0), shards)
+    at_y, at_z = hold((at_y, at_z))
+    at_zy = swap(at_y, Z_LO)
+    split = 3 * got.shape[0]
+    here, to_y, to_z = through_expert(
+        [got, at_y, at_z], [f32, f32, bf16], weights, [x[:split] for x in slopes], capacity
+    )
+    (to_zy,) = through_expert([at_zy], [bf16], weights, [x[split:] for x in slopes], capacity)
+    from_zy = swap(to_zy, Z_LO)
+    from_y = swap((to_y + from_zy.astype(f32)).astype(bf16), Y_HI)
+    from_z = swap(to_z, Z_LO)
+    done = (here + from_z.astype(f32) + from_y.astype(f32)).astype(bf16)
+    done, arrive, grad, gates, back_table = hold(
+        (done, arrive, grad, forward_gates[0], back_table)
+    )
+    grad_wide = grad.astype(f32)
+    back = across_experts(done, shards)
     sums = jnp.dot(back_table, back, preferred_element_type=f32)
-    gates = forward_gates[0]
     forward_out = (
         arrive.astype(f32)
         + gates[:, 0:1] * sums[:tokens]

time: 188 us -> 177 us (0.941)
  the two profiles are of different devices: /device:TPU:64 before, /device:TPU:90 now
where the time goes in v2:
time: 177 us; the launch traced here: 176 us
  waiting for transfers between devices  81.4 us (46%)
  starting transfers between devices  78.2 us (44%)
  Pallas kernels  7.61 us (4%)
  other arithmetic  3.68 us (2%)
  local copies, waits for them, and re-layouts  2.03 us (1%)
  matrix products  1.81 us (1%)
    all_to_all x2, waiting for transfers between devices, across_experts(): lax.all_to_all(x, 'expert', split_axis=0, concat_axis=0, tiled=True, axis...  52.6 us
    all_to_all x2, starting transfers between devices, across_experts(): lax.all_to_all(x, 'expert', split_axis=0, concat_axis=0, tiled=True, axis...  37.4 us
    ppermute x10, starting transfers between devices, swap(): return lax.ppermute(x, 'expert', [(i, i ^ bit) for i in range(count)])  35 us
    ppermute x10, waiting for transfers between devices, swap(): return lax.ppermute(x, 'expert', [(i, i ^ bit) for i in range(count)])  24.9 us
    pallas_call x2, Pallas kernels, through_expert(): pl.pallas_call(functools.partial(expert_kernel, blocks, capacity), out_sh...  7.61 us
    ppermute x2, starting transfers between devices, from_behind(): return lax.ppermute(x, axis, [(i, (i + by) % count) for i in range(count)])  5.84 us
    ppermute x2, waiting for transfers between devices, from_behind(): return lax.ppermute(x, axis, [(i, (i + by) % count) for i in range(count)])  3.94 us
  transfers between devices with their start and end apart: 14, of which 7 were waited for; matrix products, arithmetic and copies ran while one was open for 2% of the time, Pallas kernels for 3%

profile of v2, /device:TPU:90, one launch (start us, length us, event | category | flops | bytes accessed | tf_op | source)
XLA Modules:
  0.0 175.9 jit_solution(10666786159527067564)
XLA Ops:
  0.6 3.1 %collective-permute-start = (bf16[16,3584]{1,0:T(8,128)(2,1)}, bf16[16,3584]{1,0:T(8,128)(2,1)S(1)}, u32[]{:S(2)}, u32[]{:S(2)}) collective-permute-start(bf16[16,3584]{1,0:T(8,128)(2,1)} %bitcast.75), channel_id=1, source_target_pairs={{0,64},{64,128},{128,192},{192,256},{256,320},{320,384},{384,448},... | collective-permute-start | bytes 344072 | tf_op jit(solution)/shard_map/ppermute | solution.py:18
  3.7 2.8 %collective-permute-start.1 = (bf16[16,3584]{1,0:T(8,128)(2,1)}, bf16[16,3584]{1,0:T(8,128)(2,1)S(1)}, u32[]{:S(2)}, u32[]{:S(2)}) collective-permute-start(bf16[16,3584]{1,0:T(8,128)(2,1)} %bitcast.74), channel_id=1, source_target_pairs={{0,960},{64,0},{128,64},{192,128},{256,192},{320,256},{384,320},{4... | collective-permute-start | bytes 344072 | tf_op jit(solution)/shard_map/ppermute | solution.py:18
  6.5 0.7 copy-done.7
  7.2 0.7 copy-done.6
  7.9 0.6 multiply_reduce_fusion.1
  9.0 0.3 copy-done.8
  9.4 3.9 %collective-permute-done.1 = bf16[16,3584]{1,0:T(8,128)(2,1)S(1)} collective-permute-done((bf16[16,3584]{1,0:T(8,128)(2,1)}, bf16[16,3584]{1,0:T(8,128)(2,1)S(1)}, u32[]{:S(2)}, u32[]{:S(2)}) %collective-permute-start.1) | collective-permute-done | bytes 114720 | tf_op jit(solution)/shard_map/ppermute | solution.py:18
  13.4 1.0 fusion
  14.5 17.9 %all-to-all-start = ((bf16[8,8,3584]{2,1,0:T(8,128)(2,1)}), bf16[8,8,3584]{2,1,0:T(8,128)(2,1)S(1)}, u32[]{:S(2)}, u32[]{:S(2)}) async-start(bf16[8,8,3584]{2,1,0:T(8,128)(2,1)} %fusion), calls=%async_computation | async-start | bytes 917504 | tf_op jit(solution)/shard_map/all_to_all | solution.py:28
  32.4 0.9 pad_maximum_fusion
  33.3 25.6 %all-to-all-done = bf16[8,8,3584]{2,1,0:T(8,128)(2,1)S(1)} async-done(((bf16[8,8,3584]{2,1,0:T(8,128)(2,1)}), bf16[8,8,3584]{2,1,0:T(8,128)(2,1)S(1)}, u32[]{:S(2)}, u32[]{:S(2)}) %all-to-all-start) | async-done | bytes 458784 | tf_op jit(solution)/shard_map/all_to_all | solution.py:28
  58.9 2.0 %collective-permute-start.3 = (bf16[64,3584]{1,0:T(8,128)(2,1)S(1)}, bf16[64,3584]{1,0:T(8,128)(2,1)S(1)}, u32[]{:S(2)}, u32[]{:S(2)}) collective-permute-start(bf16[64,3584]{1,0:T(8,128)(2,1)S(1)} %bitcast.57), channel_id=1, source_target_pairs={{0,4},{1,5},{2,6},{3,7},{4,0},{5,1},{6,2},{7,3},{8,12},{9,13},{10,... | collective-permute-start | bytes 1376264 | tf_op jit(solution)/shard_map/ppermute | solution.py:23
  60.9 7.7 %collective-permute-start.2 = (bf16[64,3584]{1,0:T(8,128)(2,1)S(1)}, bf16[64,3584]{1,0:T(8,128)(2,1)S(1)}, u32[]{:S(2)}, u32[]{:S(2)}) collective-permute-start(bf16[64,3584]{1,0:T(8,128)(2,1)S(1)} %bitcast.58), channel_id=1, source_target_pairs={{0,2},{1,3},{2,0},{3,1},{4,6},{5,7},{6,4},{7,5},{8,10},{9,11},{10,... | collective-permute-start | bytes 1376264 | tf_op jit(solution)/shard_map/ppermute | solution.py:23
  68.7 1.9 %collective-permute-start.4 = (bf16[3584,128]{1,0:T(8,128)(2,1)S(1)}, bf16[3584,128]{1,0:T(8,128)(2,1)S(1)}, u32[]{:S(2)}, u32[]{:S(2)}) collective-permute-start(bf16[3584,128]{1,0:T(8,128)(2,1)S(1)} %bitcast.48), channel_id=1, source_target_pairs={{0,1},{1,0},{2,3},{3,2},{4,5},{5,4},{6,7},{7,6},{8,9},{9,8},{10,11... | collective-permute-start | bytes 2752520 | tf_op jit(solution)/shard_map/ppermute | solution.py:23
  70.6 2.4 %collective-permute-start.5 = (bf16[3584,128]{1,0:T(8,128)(2,1)S(1)}, bf16[3584,128]{1,0:T(8,128)(2,1)S(1)}, u32[]{:S(2)}, u32[]{:S(2)}) collective-permute-start(bf16[3584,128]{1,0:T(8,128)(2,1)S(1)} %bitcast.51), channel_id=1, source_target_pairs={{0,1},{1,0},{2,3},{3,2},{4,5},{5,4},{6,7},{7,6},{8,9},{9,8},{10,11... | collective-permute-start | bytes 2752520 | tf_op jit(solution)/shard_map/ppermute | solution.py:23
  73.0 1.9 %collective-permute-start.6 = (bf16[128,3584]{1,0:T(8,128)(2,1)S(1)}, bf16[128,3584]{1,0:T(8,128)(2,1)S(1)}, u32[]{:S(2)}, u32[]{:S(2)}) collective-permute-start(bf16[128,3584]{1,0:T(8,128)(2,1)S(1)} %bitcast.54), channel_id=1, source_target_pairs={{0,1},{1,0},{2,3},{3,2},{4,5},{5,4},{6,7},{7,6},{8,9},{9,8},{10,11... | collective-permute-start | bytes 2752520 | tf_op jit(solution)/shard_map/ppermute | solution.py:23
  75.5 2.4 %collective-permute-start.7 = (bf16[256,256]{1,0:T(8,128)(2,1)S(1)}, bf16[256,256]{1,0:T(8,128)(2,1)S(1)}, u32[]{:S(2)}, u32[]{:S(2)}) collective-permute-start(bf16[256,256]{1,0:T(8,128)(2,1)S(1)} %convolution_convert_fusion.1), channel_id=1, source_target_pairs={{0,1},{1,0},{2,3},{3,2},{4,5},{5,4},{6,7},{7,6},{8,9},{9,8},{10,11... | collective-permute-start | bytes 393224 | tf_op jit(solution)/shard_map/ppermute | solution.py:23
  77.9 5.5 %collective-permute-done.2.refs_1_ = bf16[64,3584]{1,0:T(8,128)(2,1)S(1)} collective-permute-done((bf16[64,3584]{1,0:T(8,128)(2,1)S(1)}, bf16[64,3584]{1,0:T(8,128)(2,1)S(1)}, u32[]{:S(2)}, u32[]{:S(2)}) %collective-permute-start.2) | collective-permute-done | bytes 458784 | tf_op jit(solution)/shard_map/ppermute | solution.py:23
  83.4 3.6 %collective-permute-start.9 = (bf16[64,3584]{1,0:T(8,128)(2,1)S(1)}, bf16[64,3584]{1,0:T(8,128)(2,1)S(1)}, u32[]{:S(2)}, u32[]{:S(2)}) collective-permute-start(bf16[64,3584]{1,0:T(8,128)(2,1)S(1)} %collective-permute-done.2.refs_1_), channel_id=1, source_target_pairs={{0,4},{1,5},{2,6},{3,7},{4,0},{5,1},{6,2},{7,3},{8,12},{9,13},{10,... | collective-permute-start | bytes 1376264 | tf_op jit(solution)/shard_map/ppermute | solution.py:23
  87.2 6.5 %collective-permute-done.9.refs_0_ = bf16[64,3584]{1,0:T(8,128)(2,1)S(1)} collective-permute-done((bf16[64,3584]{1,0:T(8,128)(2,1)S(1)}, bf16[64,3584]{1,0:T(8,128)(2,1)S(1)}, u32[]{:S(2)}, u32[]{:S(2)}) %collective-permute-start.9) | collective-permute-done | bytes 458784 | tf_op jit(solution)/shard_map/ppermute | solution.py:23
  93.7 2.8 %shard_map.195 = bf16[64,3584]{1,0:T(8,128)(2,1)S(1)} custom-call(bf16[64,3584]{1,0:T(8,128)(2,1)S(1)} %collective-permute-done.9.refs_0_, bf16[3584,128]{1,0:T(8,128)(2,1)S(1)} %bitcast.49, bf16[3584,128]{1,0:T(8,128)(2,1)S(1)} %collective-permute-done.4.refs_4_.refs_2_, bf16[3584,128]{1,0:T(8,128)(2,1)S(1)} %bitcast.52, ...), custom_call_target="tpu_custom_call" | custom-call | flops 704643072 | bytes 6881280 | tf_op jit(solution)/shard_map/pallas_call | solution.py:99
  96.6 3.6 %collective-permute-start.10 = (bf16[64,3584]{1,0:T(8,128)(2,1)S(1)}, bf16[64,3584]{1,0:T(8,128)(2,1)S(1)}, u32[]{:S(2)}, u32[]{:S(2)}) collective-permute-start(bf16[64,3584]{1,0:T(8,128)(2,1)S(1)} %shard_map.195), channel_id=1, source_target_pairs={{0,4},{1,5},{2,6},{3,7},{4,0},{5,1},{6,2},{7,3},{8,12},{9,13},{10,... | collective-permute-start | bytes 1376264 | tf_op jit(solution)/shard_map/ppermute | solution.py:23
  100.3 4.8 %shard_map.194 = (f32[64,3584]{1,0:T(8,128)S(1)}, f32[64,3584]{1,0:T(8,128)S(1)}, bf16[64,3584]{1,0:T(8,128)(2,1)S(1)}) custom-call(bf16[64,3584]{1,0:T(8,128)(2,1)S(1)} %bitcast.59, bf16[64,3584]{1,0:T(8,128)(2,1)S(1)} %collective-permute-done.2.refs_1_, bf16[64,3584]{1,0:T(8,128)(2,1)S(1)} %collective-permute-done.3.refs_2_, ...), custom_call_target="tpu_custom_call" | custom-call | flops 2113929216 | bytes 9633792 | tf_op jit(solution)/shard_map/pallas_call | solution.py:99
  105.1 2.2 %collective-permute-start.8 = (bf16[64,3584]{1,0:T(8,128)(2,1)S(1)}, bf16[64,3584]{1,0:T(8,128)(2,1)S(1)}, u32[]{:S(2)}, u32[]{:S(2)}) collective-permute-start(bf16[64,3584]{1,0:T(8,128)(2,1)S(1)} %get-tuple-element.32), channel_id=1, source_target_pairs={{0,4},{1,5},{2,6},{3,7},{4,0},{5,1},{6,2},{7,3},{8,12},{9,13},{10,... | collective-permute-start | bytes 1376264 | tf_op jit(solution)/shard_map/ppermute | solution.py:23
  107.3 3.6 %collective-permute-done.10 = bf16[64,3584]{1,0:T(8,128)(2,1)S(1)} collective-permute-done((bf16[64,3584]{1,0:T(8,128)(2,1)S(1)}, bf16[64,3584]{1,0:T(8,128)(2,1)S(1)}, u32[]{:S(2)}, u32[]{:S(2)}) %collective-permute-start.10) | collective-permute-done | bytes 458784 | tf_op jit(solution)/shard_map/ppermute | solution.py:23
  111.0 7.1 %collective-permute-start.11 = (bf16[64,3584]{1,0:T(8,128)(2,1)S(1)}, bf16[64,3584]{1,0:T(8,128)(2,1)S(1)}, u32[]{:S(2)}, u32[]{:S(2)}) collective-permute-start(bf16[64,3584]{1,0:T(8,128)(2,1)S(1)} %add_convert_fusion.1), channel_id=1, source_target_pairs={{0,2},{1,3},{2,0},{3,1},{4,6},{5,7},{6,4},{7,5},{8,10},{9,11},{10,... | collective-permute-start | bytes 1376264 | tf_op jit(solution)/shard_map/ppermute | solution.py:23
  118.1 9.3 %collective-permute-done.11 = bf16[64,3584]{1,0:T(8,128)(2,1)S(1)} collective-permute-done((bf16[64,3584]{1,0:T(8,128)(2,1)S(1)}, bf16[64,3584]{1,0:T(8,128)(2,1)S(1)}, u32[]{:S(2)}, u32[]{:S(2)}) %collective-permute-start.11) | collective-permute-done | bytes 458784 | tf_op jit(solution)/shard_map/ppermute | solution.py:23
  127.4 0.9 add_convert_fusion
  128.3 19.6 %all-to-all-start.1 = ((bf16[8,8,3584]{2,1,0:T(8,128)(2,1)}), bf16[8,8,3584]{2,1,0:T(8,128)(2,1)S(1)}, u32[]{:S(2)}, u32[]{:S(2)}) async-start(bf16[8,8,3584]{2,1,0:T(8,128)(2,1)} %bitcast.26), calls=%async_computation.1 | async-start | bytes 917504 | tf_op jit(solution)/shard_map/all_to_all | solution.py:28
  147.9 27.0 %all-to-all-done.1 = bf16[8,8,3584]{2,1,0:T(8,128)(2,1)S(1)} async-done(((bf16[8,8,3584]{2,1,0:T(8,128)(2,1)}), bf16[8,8,3584]{2,1,0:T(8,128)(2,1)S(1)}, u32[]{:S(2)}, u32[]{:S(2)}) %all-to-all-start.1) | async-done | bytes 458784 | tf_op jit(solution)/shard_map/all_to_all | solution.py:28
  174.9 0.3 fusion.1
  175.2 0.8 fusion.28
  (64 shorter events, 1.4 us)
Async XLA Ops:
  0.6 12.8 %collective-permute-start = (bf16[16,3584]{1,0:T(8,128)(2,1)}, bf16[16,3584]{1,0:T(8,128)(2,1)S(1)}, u32[]{:S(2)}, u32[]{:S(2)}) collective-permute-start(bf16[16,3584]{1,0:T(8,128)(2,1)} %bitcast.75), channel_id=1, source_target_pairs={{0,64},{64,128},{128,192},{192,256},{256,320},{320,384},{384,448},... | collective-permute-start | bytes 344072 | tf_op jit(solution)/shard_map/ppermute | solution.py:18
  3.7 9.6 %collective-permute-start.1 = (bf16[16,3584]{1,0:T(8,128)(2,1)}, bf16[16,3584]{1,0:T(8,128)(2,1)S(1)}, u32[]{:S(2)}, u32[]{:S(2)}) collective-permute-start(bf16[16,3584]{1,0:T(8,128)(2,1)} %bitcast.74), channel_id=1, source_target_pairs={{0,960},{64,0},{128,64},{192,128},{256,192},{320,256},{384,320},{4... | collective-permute-start | bytes 344072 | tf_op jit(solution)/shard_map/ppermute | solution.py:18
  6.5 0.7 copy-start.7
  7.2 0.7 copy-start.6
  8.5 23.8 %copy-start.5 = (bf16[1,256,128]{2,1,0:T(8,128)(2,1)S(1)}, bf16[1,256,128]{2,1,0:T(8,128)(2,1)}, u32[]{:S(2)}) copy-start(bf16[1,256,128]{2,1,0:T(8,128)(2,1)} %param.29) | copy-start | bytes 196612
  8.7 0.7 copy-start.8
  8.7 64.3 %copy-start.2 = (bf16[1,128,3584]{2,1,0:T(8,128)(2,1)S(1)}, bf16[1,128,3584]{2,1,0:T(8,128)(2,1)}, u32[]{:S(2)}) copy-start(bf16[1,128,3584]{2,1,0:T(8,128)(2,1)} %param.27) | copy-start | bytes 2752516
  13.4 1.1 copy-start.3
  13.4 55.2 %copy-start = (bf16[1,3584,128]{2,1,0:T(8,128)(2,1)S(1)}, bf16[1,3584,128]{2,1,0:T(8,128)(2,1)}, u32[]{:S(2)}) copy-start(bf16[1,3584,128]{2,1,0:T(8,128)(2,1)} %param.25) | copy-start | bytes 2752516
  13.4 57.2 %copy-start.1 = (bf16[1,3584,128]{2,1,0:T(8,128)(2,1)S(1)}, bf16[1,3584,128]{2,1,0:T(8,128)(2,1)}, u32[]{:S(2)}) copy-start(bf16[1,3584,128]{2,1,0:T(8,128)(2,1)} %param.26) | copy-start | bytes 2752516
  14.5 44.4 %all-to-all-start = ((bf16[8,8,3584]{2,1,0:T(8,128)(2,1)}), bf16[8,8,3584]{2,1,0:T(8,128)(2,1)S(1)}, u32[]{:S(2)}, u32[]{:S(2)}) async-start(bf16[8,8,3584]{2,1,0:T(8,128)(2,1)} %fusion), calls=%async_computation | async-start | bytes 917504 | tf_op jit(solution)/shard_map/all_to_all | solution.py:28
  32.3 0.9 copy-start.10
  32.3 0.9 copy-start.11
  32.4 0.9 copy-start.12
  58.9 16.1 %copy-start.13 = (pred[256]{0:T(512)(128)(4,1)S(1)}, pred[256]{0:T(512)(128)(4,1)}, u32[]{:S(2)}) copy-start(pred[256]{0:T(512)(128)(4,1)} %constant.73) | copy-start | bytes 772
  58.9 16.6 %collective-permute-start.3 = (bf16[64,3584]{1,0:T(8,128)(2,1)S(1)}, bf16[64,3584]{1,0:T(8,128)(2,1)S(1)}, u32[]{:S(2)}, u32[]{:S(2)}) collective-permute-start(bf16[64,3584]{1,0:T(8,128)(2,1)S(1)} %bitcast.57), channel_id=1, source_target_pairs={{0,4},{1,5},{2,6},{3,7},{4,0},{5,1},{6,2},{7,3},{8,12},{9,13},{10,... | collective-permute-start | bytes 1376264 | tf_op jit(solution)/shard_map/ppermute | solution.py:23
  60.9 22.4 %collective-permute-start.2 = (bf16[64,3584]{1,0:T(8,128)(2,1)S(1)}, bf16[64,3584]{1,0:T(8,128)(2,1)S(1)}, u32[]{:S(2)}, u32[]{:S(2)}) collective-permute-start(bf16[64,3584]{1,0:T(8,128)(2,1)S(1)} %bitcast.58), channel_id=1, source_target_pairs={{0,2},{1,3},{2,0},{3,1},{4,6},{5,7},{6,4},{7,5},{8,10},{9,11},{10,... | collective-permute-start | bytes 1376264 | tf_op jit(solution)/shard_map/ppermute | solution.py:23
  68.7 25.1 %collective-permute-start.4 = (bf16[3584,128]{1,0:T(8,128)(2,1)S(1)}, bf16[3584,128]{1,0:T(8,128)(2,1)S(1)}, u32[]{:S(2)}, u32[]{:S(2)}) collective-permute-start(bf16[3584,128]{1,0:T(8,128)(2,1)S(1)} %bitcast.48), channel_id=1, source_target_pairs={{0,1},{1,0},{2,3},{3,2},{4,5},{5,4},{6,7},{7,6},{8,9},{9,8},{10,11... | collective-permute-start | bytes 2752520 | tf_op jit(solution)/shard_map/ppermute | solution.py:23
  70.6 23.1 %collective-permute-start.5 = (bf16[3584,128]{1,0:T(8,128)(2,1)S(1)}, bf16[3584,128]{1,0:T(8,128)(2,1)S(1)}, u32[]{:S(2)}, u32[]{:S(2)}) collective-permute-start(bf16[3584,128]{1,0:T(8,128)(2,1)S(1)} %bitcast.51), channel_id=1, source_target_pairs={{0,1},{1,0},{2,3},{3,2},{4,5},{5,4},{6,7},{7,6},{8,9},{9,8},{10,11... | collective-permute-start | bytes 2752520 | tf_op jit(solution)/shard_map/ppermute | solution.py:23
  73.0 20.7 %collective-permute-start.6 = (bf16[128,3584]{1,0:T(8,128)(2,1)S(1)}, bf16[128,3584]{1,0:T(8,128)(2,1)S(1)}, u32[]{:S(2)}, u32[]{:S(2)}) collective-permute-start(bf16[128,3584]{1,0:T(8,128)(2,1)S(1)} %bitcast.54), channel_id=1, source_target_pairs={{0,1},{1,0},{2,3},{3,2},{4,5},{5,4},{6,7},{7,6},{8,9},{9,8},{10,11... | collective-permute-start | bytes 2752520 | tf_op jit(solution)/shard_map/ppermute | solution.py:23
  75.5 11.5 %collective-permute-start.7 = (bf16[256,256]{1,0:T(8,128)(2,1)S(1)}, bf16[256,256]{1,0:T(8,128)(2,1)S(1)}, u32[]{:S(2)}, u32[]{:S(2)}) collective-permute-start(bf16[256,256]{1,0:T(8,128)(2,1)S(1)} %convolution_convert_fusion.1), channel_id=1, source_target_pairs={{0,1},{1,0},{2,3},{3,2},{4,5},{5,4},{6,7},{7,6},{8,9},{9,8},{10,11... | collective-permute-start | bytes 393224 | tf_op jit(solution)/shard_map/ppermute | solution.py:23
  83.4 10.4 %collective-permute-start.9 = (bf16[64,3584]{1,0:T(8,128)(2,1)S(1)}, bf16[64,3584]{1,0:T(8,128)(2,1)S(1)}, u32[]{:S(2)}, u32[]{:S(2)}) collective-permute-start(bf16[64,3584]{1,0:T(8,128)(2,1)S(1)} %collective-permute-done.2.refs_1_), channel_id=1, source_target_pairs={{0,4},{1,5},{2,6},{3,7},{4,0},{5,1},{6,2},{7,3},{8,12},{9,13},{10,... | collective-permute-start | bytes 1376264 | tf_op jit(solution)/shard_map/ppermute | solution.py:23
  96.6 14.3 %collective-permute-start.10 = (bf16[64,3584]{1,0:T(8,128)(2,1)S(1)}, bf16[64,3584]{1,0:T(8,128)(2,1)S(1)}, u32[]{:S(2)}, u32[]{:S(2)}) collective-permute-start(bf16[64,3584]{1,0:T(8,128)(2,1)S(1)} %shard_map.195), channel_id=1, source_target_pairs={{0,4},{1,5},{2,6},{3,7},{4,0},{5,1},{6,2},{7,3},{8,12},{9,13},{10,... | collective-permute-start | bytes 1376264 | tf_op jit(solution)/shard_map/ppermute | solution.py:23
  105.1 13.0 %collective-permute-start.8 = (bf16[64,3584]{1,0:T(8,128)(2,1)S(1)}, bf16[64,3584]{1,0:T(8,128)(2,1)S(1)}, u32[]{:S(2)}, u32[]{:S(2)}) collective-permute-start(bf16[64,3584]{1,0:T(8,128)(2,1)S(1)} %get-tuple-element.32), channel_id=1, source_target_pairs={{0,4},{1,5},{2,6},{3,7},{4,0},{5,1},{6,2},{7,3},{8,12},{9,13},{10,... | collective-permute-start | bytes 1376264 | tf_op jit(solution)/shard_map/ppermute | solution.py:23
  111.0 16.4 %collective-permute-start.11 = (bf16[64,3584]{1,0:T(8,128)(2,1)S(1)}, bf16[64,3584]{1,0:T(8,128)(2,1)S(1)}, u32[]{:S(2)}, u32[]{:S(2)}) collective-permute-start(bf16[64,3584]{1,0:T(8,128)(2,1)S(1)} %add_convert_fusion.1), channel_id=1, source_target_pairs={{0,2},{1,3},{2,0},{3,1},{4,6},{5,7},{6,4},{7,5},{8,10},{9,11},{10,... | collective-permute-start | bytes 1376264 | tf_op jit(solution)/shard_map/ppermute | solution.py:23
  128.3 19.6 %copy-start.9 = (f32[1,16,2]{1,2,0:T(2,128)S(1)}, f32[1,16,2]{1,2,0:T(2,128)}, u32[]{:S(2)}) copy-start(f32[1,16,2]{1,2,0:T(2,128)} %param.23) | copy-start | bytes 388
  128.3 46.6 %all-to-all-start.1 = ((bf16[8,8,3584]{2,1,0:T(8,128)(2,1)}), bf16[8,8,3584]{2,1,0:T(8,128)(2,1)S(1)}, u32[]{:S(2)}, u32[]{:S(2)}) async-start(bf16[8,8,3584]{2,1,0:T(8,128)(2,1)} %bitcast.26), calls=%async_computation.1 | async-start | bytes 917504 | tf_op jit(solution)/shard_map/all_to_all | solution.py:28
  147.9 27.3 %copy-start.4 = (bf16[16,3584]{1,0:T(8,128)(2,1)S(1)}, bf16[16,3584]{1,0:T(8,128)(2,1)}, u32[]{:S(2)}) copy-start(bf16[16,3584]{1,0:T(8,128)(2,1)} %copy-done.3) | copy-start | bytes 344068

commit v3 on v2

--- a/solution.py
+++ b/solution.py
@@ -156,26 +156,20 @@
     first = (((0,), (0,)), ((), ()))
     send = lax.dot_general(send_table, rows_in, first, preferred_element_type=f32).astype(bf16)
 
+    send, both_saved = hold((send, jnp.concatenate([saved_gate[0], saved_up[0]], axis=1)))
     got = across_experts(send, shards)
-
-    got, gate, up, down, both_saved = hold(
-        (
-            got,
-            gate_weight[0],
-            up_weight[0],
-            down_weight[0],
-            jnp.concatenate([saved_gate[0], saved_up[0]], axis=1),
-        )
-    )
-
-    weights = [w for mine in (gate, up, down) for w in (mine, swap(mine, CORE))]
 
     def saved_for(device):
         slot, is_back = saved_slots(device, shards, capacity)
         pick = (slot[:, None] == jnp.arange(saved_gate.shape[1])) & (is_back[:, None] == 1)
         return jnp.dot(pick.astype(bf16), both_saved, preferred_element_type=f32).astype(bf16)
 
-    saved = [saved_for(own), swap(saved_for(own ^ CORE), CORE)]
+    saved_other = swap(saved_for(own ^ CORE), CORE)
+    got, saved_other, gate, up, down = hold(
+        (got, saved_other, gate_weight[0], up_weight[0], down_weight[0])
+    )
+    weights = [w for mine in (gate, up, down) for w in (mine, swap(mine, CORE))]
+    saved = [saved_for(own), saved_other]
     g, u = (
         jnp.concatenate([x.astype(f32) for x in pair], axis=1)
         for pair in zip(*(jnp.split(x, 2, axis=1) for x in saved))

time: 177 us -> 177 us (level)
  the two profiles are of different devices: /device:TPU:90 before, /device:TPU:88 now
where the time goes in v3:
time: 177 us; the launch traced here: 176 us
  waiting for transfers between devices  82.4 us (47%)
  starting transfers between devices  76.2 us (43%)
  Pallas kernels  7.62 us (4%)
  local copies, waits for them, and re-layouts  3.91 us (2%)
  other arithmetic  2.84 us (2%)
  matrix products  1.81 us (1%)
    all_to_all x2, waiting for transfers between devices, across_experts(): lax.all_to_all(x, 'expert', split_axis=0, concat_axis=0, tiled=True, axis...  49.9 us
    all_to_all x2, starting transfers between devices, across_experts(): lax.all_to_all(x, 'expert', split_axis=0, concat_axis=0, tiled=True, axis...  36.5 us
    ppermute x10, starting transfers between devices, swap(): return lax.ppermute(x, 'expert', [(i, i ^ bit) for i in range(count)])  33.9 us
    ppermute x10, waiting for transfers between devices, swap(): return lax.ppermute(x, 'expert', [(i, i ^ bit) for i in range(count)])  29.5 us
    pallas_call x2, Pallas kernels, through_expert(): pl.pallas_call(functools.partial(expert_kernel, blocks, capacity), out_sh...  7.62 us
    ppermute x2, starting transfers between devices, from_behind(): return lax.ppermute(x, axis, [(i, (i + by) % count) for i in range(count)])  5.84 us
  transfers between devices with their start and end apart: 14, of which 8 were waited for; matrix products, arithmetic and copies ran while one was open for 2% of the time, Pallas kernels for 3%

profile of v3, /device:TPU:88, one launch (start us, length us, event | category | flops | bytes accessed | tf_op | source)
XLA Modules:
  0.0 175.8 jit_solution(10909368497619945883)
XLA Ops:
  0.6 3.1 %collective-permute-start = (bf16[16,3584]{1,0:T(8,128)(2,1)}, bf16[16,3584]{1,0:T(8,128)(2,1)S(1)}, u32[]{:S(2)}, u32[]{:S(2)}) collective-permute-start(bf16[16,3584]{1,0:T(8,128)(2,1)} %bitcast.75), channel_id=1, source_target_pairs={{0,64},{64,128},{128,192},{192,256},{256,320},{320,384},{384,448},... | collective-permute-start | bytes 344072 | tf_op jit(solution)/shard_map/ppermute | solution.py:18
  3.7 2.8 %collective-permute-start.1 = (bf16[16,3584]{1,0:T(8,128)(2,1)}, bf16[16,3584]{1,0:T(8,128)(2,1)S(1)}, u32[]{:S(2)}, u32[]{:S(2)}) collective-permute-start(bf16[16,3584]{1,0:T(8,128)(2,1)} %bitcast.74), channel_id=1, source_target_pairs={{0,960},{64,0},{128,64},{192,128},{256,192},{320,256},{384,320},{4... | collective-permute-start | bytes 344072 | tf_op jit(solution)/shard_map/ppermute | solution.py:18
  6.5 0.7 copy-done.8
  7.2 0.7 copy-done.7
  7.9 0.7 copy-done.9
  9.7 0.6 copy-done.5
  10.4 2.9 %collective-permute-done.1 = bf16[16,3584]{1,0:T(8,128)(2,1)S(1)} collective-permute-done((bf16[16,3584]{1,0:T(8,128)(2,1)}, bf16[16,3584]{1,0:T(8,128)(2,1)S(1)}, u32[]{:S(2)}, u32[]{:S(2)}) %collective-permute-start.1) | collective-permute-done | bytes 114720 | tf_op jit(solution)/shard_map/ppermute | solution.py:18
  13.5 1.0 convolution_convert_fusion
  14.5 17.9 %all-to-all-start = ((bf16[8,8,3584]{2,1,0:T(8,128)(2,1)}), bf16[8,8,3584]{2,1,0:T(8,128)(2,1)S(1)}, u32[]{:S(2)}, u32[]{:S(2)}) async-start(bf16[8,8,3584]{2,1,0:T(8,128)(2,1)} %bitcast.59), calls=%async_computation | async-start | bytes 917504 | tf_op jit(solution)/shard_map/all_to_all | solution.py:28
  32.7 1.9 %collective-permute-start.2 = (bf16[256,256]{1,0:T(8,128)(2,1)S(1)}, bf16[256,256]{1,0:T(8,128)(2,1)}, u32[]{:S(2)}, u32[]{:S(2)}) collective-permute-start(bf16[256,256]{1,0:T(8,128)(2,1)S(1)} %convolution_convert_fusion.2), channel_id=1, source_target_pairs={{0,1},{1,0},{2,3},{3,2},{4,5},{5,4},{6,7},{7,6},{8,9},{9,8},{10,11... | collective-permute-start | bytes 393224 | tf_op jit(solution)/shard_map/ppermute | solution.py:23
  34.6 1.4 collective-permute-done.2
  36.0 22.9 %all-to-all-done = bf16[8,8,3584]{2,1,0:T(8,128)(2,1)S(1)} async-done(((bf16[8,8,3584]{2,1,0:T(8,128)(2,1)}), bf16[8,8,3584]{2,1,0:T(8,128)(2,1)S(1)}, u32[]{:S(2)}, u32[]{:S(2)}) %all-to-all-start) | async-done | bytes 458784 | tf_op jit(solution)/shard_map/all_to_all | solution.py:28
  58.9 1.9 %collective-permute-start.4 = (bf16[64,3584]{1,0:T(8,128)(2,1)S(1)}, bf16[64,3584]{1,0:T(8,128)(2,1)S(1)}, u32[]{:S(2)}, u32[]{:S(2)}) collective-permute-start(bf16[64,3584]{1,0:T(8,128)(2,1)S(1)} %bitcast.56), channel_id=1, source_target_pairs={{0,4},{1,5},{2,6},{3,7},{4,0},{5,1},{6,2},{7,3},{8,12},{9,13},{10,... | collective-permute-start | bytes 1376264 | tf_op jit(solution)/shard_map/ppermute | solution.py:23
  60.9 7.7 %collective-permute-start.3 = (bf16[64,3584]{1,0:T(8,128)(2,1)S(1)}, bf16[64,3584]{1,0:T(8,128)(2,1)S(1)}, u32[]{:S(2)}, u32[]{:S(2)}) collective-permute-start(bf16[64,3584]{1,0:T(8,128)(2,1)S(1)} %bitcast.57), channel_id=1, source_target_pairs={{0,2},{1,3},{2,0},{3,1},{4,6},{5,7},{6,4},{7,5},{8,10},{9,11},{10,... | collective-permute-start | bytes 1376264 | tf_op jit(solution)/shard_map/ppermute | solution.py:23
  68.6 1.9 %collective-permute-start.5 = (bf16[3584,128]{1,0:T(8,128)(2,1)S(1)}, bf16[3584,128]{1,0:T(8,128)(2,1)S(1)}, u32[]{:S(2)}, u32[]{:S(2)}) collective-permute-start(bf16[3584,128]{1,0:T(8,128)(2,1)S(1)} %bitcast.47), channel_id=1, source_target_pairs={{0,1},{1,0},{2,3},{3,2},{4,5},{5,4},{6,7},{7,6},{8,9},{9,8},{10,11... | collective-permute-start | bytes 2752520 | tf_op jit(solution)/shard_map/ppermute | solution.py:23
  70.5 2.4 %collective-permute-start.6 = (bf16[3584,128]{1,0:T(8,128)(2,1)S(1)}, bf16[3584,128]{1,0:T(8,128)(2,1)S(1)}, u32[]{:S(2)}, u32[]{:S(2)}) collective-permute-start(bf16[3584,128]{1,0:T(8,128)(2,1)S(1)} %bitcast.50), channel_id=1, source_target_pairs={{0,1},{1,0},{2,3},{3,2},{4,5},{5,4},{6,7},{7,6},{8,9},{9,8},{10,11... | collective-permute-start | bytes 2752520 | tf_op jit(solution)/shard_map/ppermute | solution.py:23
  73.0 1.9 %collective-permute-start.7 = (bf16[128,3584]{1,0:T(8,128)(2,1)S(1)}, bf16[128,3584]{1,0:T(8,128)(2,1)S(1)}, u32[]{:S(2)}, u32[]{:S(2)}) collective-permute-start(bf16[128,3584]{1,0:T(8,128)(2,1)S(1)} %bitcast.53), channel_id=1, source_target_pairs={{0,1},{1,0},{2,3},{3,2},{4,5},{5,4},{6,7},{7,6},{8,9},{9,8},{10,11... | collective-permute-start | bytes 2752520 | tf_op jit(solution)/shard_map/ppermute | solution.py:23
  75.2 8.1 %collective-permute-done.3.refs_1_ = bf16[64,3584]{1,0:T(8,128)(2,1)S(1)} collective-permute-done((bf16[64,3584]{1,0:T(8,128)(2,1)S(1)}, bf16[64,3584]{1,0:T(8,128)(2,1)S(1)}, u32[]{:S(2)}, u32[]{:S(2)}) %collective-permute-start.3) | collective-permute-done | bytes 458784 | tf_op jit(solution)/shard_map/ppermute | solution.py:23
  83.3 3.6 %collective-permute-start.9 = (bf16[64,3584]{1,0:T(8,128)(2,1)S(1)}, bf16[64,3584]{1,0:T(8,128)(2,1)S(1)}, u32[]{:S(2)}, u32[]{:S(2)}) collective-permute-start(bf16[64,3584]{1,0:T(8,128)(2,1)S(1)} %collective-permute-done.3.refs_1_), channel_id=1, source_target_pairs={{0,4},{1,5},{2,6},{3,7},{4,0},{5,1},{6,2},{7,3},{8,12},{9,13},{10,... | collective-permute-start | bytes 1376264 | tf_op jit(solution)/shard_map/ppermute | solution.py:23
  86.9 0.9 fusion.39
  88.0 5.7 %collective-permute-done.9.refs_0_ = bf16[64,3584]{1,0:T(8,128)(2,1)S(1)} collective-permute-done((bf16[64,3584]{1,0:T(8,128)(2,1)S(1)}, bf16[64,3584]{1,0:T(8,128)(2,1)S(1)}, u32[]{:S(2)}, u32[]{:S(2)}) %collective-permute-start.9) | collective-permute-done | bytes 458784 | tf_op jit(solution)/shard_map/ppermute | solution.py:23
  93.6 2.8 %shard_map.195 = bf16[64,3584]{1,0:T(8,128)(2,1)S(1)} custom-call(bf16[64,3584]{1,0:T(8,128)(2,1)S(1)} %collective-permute-done.9.refs_0_, bf16[3584,128]{1,0:T(8,128)(2,1)S(1)} %bitcast.48, bf16[3584,128]{1,0:T(8,128)(2,1)S(1)} %collective-permute-done.5.refs_4_.refs_2_, bf16[3584,128]{1,0:T(8,128)(2,1)S(1)} %bitcast.51, ...), custom_call_target="tpu_custom_call" | custom-call | flops 704643072 | bytes 6881280 | tf_op jit(solution)/shard_map/pallas_call | solution.py:99
  96.5 3.6 %collective-permute-start.10 = (bf16[64,3584]{1,0:T(8,128)(2,1)S(1)}, bf16[64,3584]{1,0:T(8,128)(2,1)S(1)}, u32[]{:S(2)}, u32[]{:S(2)}) collective-permute-start(bf16[64,3584]{1,0:T(8,128)(2,1)S(1)} %shard_map.195), channel_id=1, source_target_pairs={{0,4},{1,5},{2,6},{3,7},{4,0},{5,1},{6,2},{7,3},{8,12},{9,13},{10,... | collective-permute-start | bytes 1376264 | tf_op jit(solution)/shard_map/ppermute | solution.py:23
  100.1 4.8 %shard_map.194 = (f32[64,3584]{1,0:T(8,128)S(1)}, f32[64,3584]{1,0:T(8,128)S(1)}, bf16[64,3584]{1,0:T(8,128)(2,1)S(1)}) custom-call(bf16[64,3584]{1,0:T(8,128)(2,1)S(1)} %bitcast.58, bf16[64,3584]{1,0:T(8,128)(2,1)S(1)} %collective-permute-done.3.refs_1_, bf16[64,3584]{1,0:T(8,128)(2,1)S(1)} %collective-permute-done.4.refs_2_, ...), custom_call_target="tpu_custom_call" | custom-call | flops 2113929216 | bytes 9633792 | tf_op jit(solution)/shard_map/pallas_call | solution.py:99
  104.9 2.2 %collective-permute-start.8 = (bf16[64,3584]{1,0:T(8,128)(2,1)S(1)}, bf16[64,3584]{1,0:T(8,128)(2,1)S(1)}, u32[]{:S(2)}, u32[]{:S(2)}) collective-permute-start(bf16[64,3584]{1,0:T(8,128)(2,1)S(1)} %get-tuple-element.36), channel_id=1, source_target_pairs={{0,4},{1,5},{2,6},{3,7},{4,0},{5,1},{6,2},{7,3},{8,12},{9,13},{10,... | collective-permute-start | bytes 1376264 | tf_op jit(solution)/shard_map/ppermute | solution.py:23
  107.2 4.1 %collective-permute-done.10 = bf16[64,3584]{1,0:T(8,128)(2,1)S(1)} collective-permute-done((bf16[64,3584]{1,0:T(8,128)(2,1)S(1)}, bf16[64,3584]{1,0:T(8,128)(2,1)S(1)}, u32[]{:S(2)}, u32[]{:S(2)}) %collective-permute-start.10) | collective-permute-done | bytes 458784 | tf_op jit(solution)/shard_map/ppermute | solution.py:23
  111.3 6.6 %collective-permute-start.11 = (bf16[64,3584]{1,0:T(8,128)(2,1)S(1)}, bf16[64,3584]{1,0:T(8,128)(2,1)S(1)}, u32[]{:S(2)}, u32[]{:S(2)}) collective-permute-start(bf16[64,3584]{1,0:T(8,128)(2,1)S(1)} %add_convert_fusion.1), channel_id=1, source_target_pairs={{0,2},{1,3},{2,0},{3,1},{4,6},{5,7},{6,4},{7,5},{8,10},{9,11},{10,... | collective-permute-start | bytes 1376264 | tf_op jit(solution)/shard_map/ppermute | solution.py:23
  118.0 10.3 %collective-permute-done.11 = bf16[64,3584]{1,0:T(8,128)(2,1)S(1)} collective-permute-done((bf16[64,3584]{1,0:T(8,128)(2,1)S(1)}, bf16[64,3584]{1,0:T(8,128)(2,1)S(1)}, u32[]{:S(2)}, u32[]{:S(2)}) %collective-permute-start.11) | collective-permute-done | bytes 458784 | tf_op jit(solution)/shard_map/ppermute | solution.py:23
  128.2 0.9 add_convert_fusion
  129.2 18.6 %all-to-all-start.1 = ((bf16[8,8,3584]{2,1,0:T(8,128)(2,1)}), bf16[8,8,3584]{2,1,0:T(8,128)(2,1)S(1)}, u32[]{:S(2)}, u32[]{:S(2)}) async-start(bf16[8,8,3584]{2,1,0:T(8,128)(2,1)} %bitcast.26), calls=%async_computation.1 | async-start | bytes 917504 | tf_op jit(solution)/shard_map/all_to_all | solution.py:28
  147.8 27.0 %all-to-all-done.1 = bf16[8,8,3584]{2,1,0:T(8,128)(2,1)S(1)} async-done(((bf16[8,8,3584]{2,1,0:T(8,128)(2,1)}), bf16[8,8,3584]{2,1,0:T(8,128)(2,1)S(1)}, u32[]{:S(2)}, u32[]{:S(2)}) %all-to-all-start.1) | async-done | bytes 458784 | tf_op jit(solution)/shard_map/all_to_all | solution.py:28
  175.1 0.8 fusion.27
  (66 shorter events, 2.3 us)
Async XLA Ops:
  0.6 12.8 %collective-permute-start = (bf16[16,3584]{1,0:T(8,128)(2,1)}, bf16[16,3584]{1,0:T(8,128)(2,1)S(1)}, u32[]{:S(2)}, u32[]{:S(2)}) collective-permute-start(bf16[16,3584]{1,0:T(8,128)(2,1)} %bitcast.75), channel_id=1, source_target_pairs={{0,64},{64,128},{128,192},{192,256},{256,320},{320,384},{384,448},... | collective-permute-start | bytes 344072 | tf_op jit(solution)/shard_map/ppermute | solution.py:18
  3.7 9.6 %collective-permute-start.1 = (bf16[16,3584]{1,0:T(8,128)(2,1)}, bf16[16,3584]{1,0:T(8,128)(2,1)S(1)}, u32[]{:S(2)}, u32[]{:S(2)}) collective-permute-start(bf16[16,3584]{1,0:T(8,128)(2,1)} %bitcast.74), channel_id=1, source_target_pairs={{0,960},{64,0},{128,64},{192,128},{256,192},{320,256},{384,320},{4... | collective-permute-start | bytes 344072 | tf_op jit(solution)/shard_map/ppermute | solution.py:18
  6.5 0.7 copy-start.8
  7.2 0.7 copy-start.7
  7.9 0.7 copy-start.9
  9.5 0.8 copy-start.5
  9.5 0.9 copy-start.6
  10.4 62.6 %copy-start.2 = (bf16[1,128,3584]{2,1,0:T(8,128)(2,1)S(1)}, bf16[1,128,3584]{2,1,0:T(8,128)(2,1)}, u32[]{:S(2)}) copy-start(bf16[1,128,3584]{2,1,0:T(8,128)(2,1)} %param.27) | copy-start | bytes 2752516
  13.3 19.1 %copy-start.11 = (s32[256]{0:T(256)S(1)}, s32[256]{0:T(256)}, u32[]{:S(2)}) copy-start(s32[256]{0:T(256)} %constant.72) | copy-start | bytes 3076
  13.3 19.1 %copy-start.12 = (s32[256]{0:T(256)S(1)}, s32[256]{0:T(256)}, u32[]{:S(2)}) copy-start(s32[256]{0:T(256)} %constant.48.clone) | copy-start | bytes 3076
  13.3 19.1 %copy-start.13 = (s32[256]{0:T(256)S(1)}, s32[256]{0:T(256)}, u32[]{:S(2)}) copy-start(s32[256]{0:T(256)} %constant.45.clone) | copy-start | bytes 3076
  13.3 19.1 %copy-start.14 = (pred[256]{0:T(512)(128)(4,1)S(1)}, pred[256]{0:T(512)(128)(4,1)}, u32[]{:S(2)}) copy-start(pred[256]{0:T(512)(128)(4,1)} %constant.73) | copy-start | bytes 772
  13.4 1.1 copy-start.3
  13.4 55.2 %copy-start = (bf16[1,3584,128]{2,1,0:T(8,128)(2,1)S(1)}, bf16[1,3584,128]{2,1,0:T(8,128)(2,1)}, u32[]{:S(2)}) copy-start(bf16[1,3584,128]{2,1,0:T(8,128)(2,1)} %param.25) | copy-start | bytes 2752516
  13.4 57.1 %copy-start.1 = (bf16[1,3584,128]{2,1,0:T(8,128)(2,1)S(1)}, bf16[1,3584,128]{2,1,0:T(8,128)(2,1)}, u32[]{:S(2)}) copy-start(bf16[1,3584,128]{2,1,0:T(8,128)(2,1)} %param.26) | copy-start | bytes 2752516
  14.5 44.4 %all-to-all-start = ((bf16[8,8,3584]{2,1,0:T(8,128)(2,1)}), bf16[8,8,3584]{2,1,0:T(8,128)(2,1)S(1)}, u32[]{:S(2)}, u32[]{:S(2)}) async-start(bf16[8,8,3584]{2,1,0:T(8,128)(2,1)} %bitcast.59), calls=%async_computation | async-start | bytes 917504 | tf_op jit(solution)/shard_map/all_to_all | solution.py:28
  32.7 3.4 %collective-permute-start.2 = (bf16[256,256]{1,0:T(8,128)(2,1)S(1)}, bf16[256,256]{1,0:T(8,128)(2,1)}, u32[]{:S(2)}, u32[]{:S(2)}) collective-permute-start(bf16[256,256]{1,0:T(8,128)(2,1)S(1)} %convolution_convert_fusion.2), channel_id=1, source_target_pairs={{0,1},{1,0},{2,3},{3,2},{4,5},{5,4},{6,7},{7,6},{8,9},{9,8},{10,11... | collective-permute-start | bytes 393224 | tf_op jit(solution)/shard_map/ppermute | solution.py:23
  58.9 16.2 %collective-permute-start.4 = (bf16[64,3584]{1,0:T(8,128)(2,1)S(1)}, bf16[64,3584]{1,0:T(8,128)(2,1)S(1)}, u32[]{:S(2)}, u32[]{:S(2)}) collective-permute-start(bf16[64,3584]{1,0:T(8,128)(2,1)S(1)} %bitcast.56), channel_id=1, source_target_pairs={{0,4},{1,5},{2,6},{3,7},{4,0},{5,1},{6,2},{7,3},{8,12},{9,13},{10,... | collective-permute-start | bytes 1376264 | tf_op jit(solution)/shard_map/ppermute | solution.py:23
  60.9 22.4 %collective-permute-start.3 = (bf16[64,3584]{1,0:T(8,128)(2,1)S(1)}, bf16[64,3584]{1,0:T(8,128)(2,1)S(1)}, u32[]{:S(2)}, u32[]{:S(2)}) collective-permute-start(bf16[64,3584]{1,0:T(8,128)(2,1)S(1)} %bitcast.57), channel_id=1, source_target_pairs={{0,2},{1,3},{2,0},{3,1},{4,6},{5,7},{6,4},{7,5},{8,10},{9,11},{10,... | collective-permute-start | bytes 1376264 | tf_op jit(solution)/shard_map/ppermute | solution.py:23
  68.6 25.0 %collective-permute-start.5 = (bf16[3584,128]{1,0:T(8,128)(2,1)S(1)}, bf16[3584,128]{1,0:T(8,128)(2,1)S(1)}, u32[]{:S(2)}, u32[]{:S(2)}) collective-permute-start(bf16[3584,128]{1,0:T(8,128)(2,1)S(1)} %bitcast.47), channel_id=1, source_target_pairs={{0,1},{1,0},{2,3},{3,2},{4,5},{5,4},{6,7},{7,6},{8,9},{9,8},{10,11... | collective-permute-start | bytes 2752520 | tf_op jit(solution)/shard_map/ppermute | solution.py:23
  70.5 23.1 %collective-permute-start.6 = (bf16[3584,128]{1,0:T(8,128)(2,1)S(1)}, bf16[3584,128]{1,0:T(8,128)(2,1)S(1)}, u32[]{:S(2)}, u32[]{:S(2)}) collective-permute-start(bf16[3584,128]{1,0:T(8,128)(2,1)S(1)} %bitcast.50), channel_id=1, source_target_pairs={{0,1},{1,0},{2,3},{3,2},{4,5},{5,4},{6,7},{7,6},{8,9},{9,8},{10,11... | collective-permute-start | bytes 2752520 | tf_op jit(solution)/shard_map/ppermute | solution.py:23
  73.0 20.7 %collective-permute-start.7 = (bf16[128,3584]{1,0:T(8,128)(2,1)S(1)}, bf16[128,3584]{1,0:T(8,128)(2,1)S(1)}, u32[]{:S(2)}, u32[]{:S(2)}) collective-permute-start(bf16[128,3584]{1,0:T(8,128)(2,1)S(1)} %bitcast.53), channel_id=1, source_target_pairs={{0,1},{1,0},{2,3},{3,2},{4,5},{5,4},{6,7},{7,6},{8,9},{9,8},{10,11... | collective-permute-start | bytes 2752520 | tf_op jit(solution)/shard_map/ppermute | solution.py:23
  83.3 10.4 %collective-permute-start.9 = (bf16[64,3584]{1,0:T(8,128)(2,1)S(1)}, bf16[64,3584]{1,0:T(8,128)(2,1)S(1)}, u32[]{:S(2)}, u32[]{:S(2)}) collective-permute-start(bf16[64,3584]{1,0:T(8,128)(2,1)S(1)} %collective-permute-done.3.refs_1_), channel_id=1, source_target_pairs={{0,4},{1,5},{2,6},{3,7},{4,0},{5,1},{6,2},{7,3},{8,12},{9,13},{10,... | collective-permute-start | bytes 1376264 | tf_op jit(solution)/shard_map/ppermute | solution.py:23
  96.5 14.8 %collective-permute-start.10 = (bf16[64,3584]{1,0:T(8,128)(2,1)S(1)}, bf16[64,3584]{1,0:T(8,128)(2,1)S(1)}, u32[]{:S(2)}, u32[]{:S(2)}) collective-permute-start(bf16[64,3584]{1,0:T(8,128)(2,1)S(1)} %shard_map.195), channel_id=1, source_target_pairs={{0,4},{1,5},{2,6},{3,7},{4,0},{5,1},{6,2},{7,3},{8,12},{9,13},{10,... | collective-permute-start | bytes 1376264 | tf_op jit(solution)/shard_map/ppermute | solution.py:23
  104.9 13.0 %collective-permute-start.8 = (bf16[64,3584]{1,0:T(8,128)(2,1)S(1)}, bf16[64,3584]{1,0:T(8,128)(2,1)S(1)}, u32[]{:S(2)}, u32[]{:S(2)}) collective-permute-start(bf16[64,3584]{1,0:T(8,128)(2,1)S(1)} %get-tuple-element.36), channel_id=1, source_target_pairs={{0,4},{1,5},{2,6},{3,7},{4,0},{5,1},{6,2},{7,3},{8,12},{9,13},{10,... | collective-permute-start | bytes 1376264 | tf_op jit(solution)/shard_map/ppermute | solution.py:23
  111.3 16.9 %collective-permute-start.11 = (bf16[64,3584]{1,0:T(8,128)(2,1)S(1)}, bf16[64,3584]{1,0:T(8,128)(2,1)S(1)}, u32[]{:S(2)}, u32[]{:S(2)}) collective-permute-start(bf16[64,3584]{1,0:T(8,128)(2,1)S(1)} %add_convert_fusion.1), channel_id=1, source_target_pairs={{0,2},{1,3},{2,0},{3,1},{4,6},{5,7},{6,4},{7,5},{8,10},{9,11},{10,... | collective-permute-start | bytes 1376264 | tf_op jit(solution)/shard_map/ppermute | solution.py:23
  129.2 18.6 %copy-start.10 = (f32[1,16,2]{1,2,0:T(2,128)S(1)}, f32[1,16,2]{1,2,0:T(2,128)}, u32[]{:S(2)}) copy-start(f32[1,16,2]{1,2,0:T(2,128)} %param.23) | copy-start | bytes 388
  129.2 45.6 %all-to-all-start.1 = ((bf16[8,8,3584]{2,1,0:T(8,128)(2,1)}), bf16[8,8,3584]{2,1,0:T(8,128)(2,1)S(1)}, u32[]{:S(2)}, u32[]{:S(2)}) async-start(bf16[8,8,3584]{2,1,0:T(8,128)(2,1)} %bitcast.26), calls=%async_computation.1 | async-start | bytes 917504 | tf_op jit(solution)/shard_map/all_to_all | solution.py:28
  147.8 27.3 %copy-start.4 = (bf16[16,3584]{1,0:T(8,128)(2,1)S(1)}, bf16[16,3584]{1,0:T(8,128)(2,1)}, u32[]{:S(2)}) copy-start(bf16[16,3584]{1,0:T(8,128)(2,1)} %copy-done.3) | copy-start | bytes 344068
